TPU v7x, 32 devices: a whole 2x2x4 slice. The times are simulated.
32 devices in a mesh: tile: 8 (over y, x, core), kern: 4 (over z).
Axes of the slice: x: 2, y: 2, z: 4, core: 2. Of those that a mesh axis runs over, the one named last changes fastest.
Arguments:
- mask_pixels: bfloat16 [1152, 9216], P(None, 'tile'), may hold values from -6 to 6
- orientation: int32 [8, 2], P('tile'), may hold values 0 or 1
- target_pattern: int32 [1152, 9216], P('kern', 'tile'), may hold values 0 or 1
- kernel_real: float32 [4, 64, 64], P('kern'), may hold values from -6 to 6
- kernel_imag: float32 [4, 64, 64], P('kern'), may hold values from -6 to 6
- eigen_weights: float32 [4], P('kern'), may hold values from 0.01 to 0.1
Outputs:
- mask_gradient: float32 [1152, 9216], P('kern', 'tile')
Inputs may be any that keep to these rules, and one draw needn't show every extreme that they name: `orientation`: 1 takes the neighbour's facing strip in order, 0 reversed; the entry for a side without neighbour is unused.
All inputs are finite; a program needn't handle non-finite values. No bound on the sum of `orientation` or of `target_pattern` on one device may be relied on, other than what follows from the above.
Results may differ from a plain program's by a relative error of at most 0.018.
Values may be sent and summed in bfloat16 or wider, within the bound.
No kernel may reach another device: no remote copies, remote signals or barrier semaphores. Data moves between devices by JAX's collectives and lax.ppermute only.
A program may use at most 64 MiB of HBM per device.

v0:
```python
import functools
import math

import jax
import jax.numpy as jnp
import ml_dtypes
import numpy as np
from jax import lax
from jax.experimental import pallas as pl
from jax.experimental.pallas import tpu as pltpu
from jax.sharding import PartitionSpec as P

N = 1152
HALO = 64
KF = 64
NE = 1280
LANES = 128
PAIR = 2 * KF
BLOCKS = N // LANES
EDGE = PAIR
PACK = EDGE + KF + 16
BF16 = jnp.bfloat16
F32 = jnp.float32
VMEM_LIMIT = 32 * 1024 * 1024


def wave_tables():
    position = np.arange(NE)[:, None]
    frequency = np.arange(KF)[None, :] - KF // 2
    phase = np.mod(position * frequency, NE).astype(np.float64) * (2.0 * math.pi / NE)
    return np.cos(phase).astype(np.float32), np.sin(phase).astype(np.float32)


def transform_tables():
    cos, sin = wave_tables()
    full = np.concatenate([cos, sin], 1)
    mid = full[HALO : HALO + N]
    ct, st = cos[HALO : HALO + N].T, sin[HALO : HALO + N].T
    columns = np.concatenate(
        [
            np.stack([ct.reshape(KF, BLOCKS, LANES), st.reshape(KF, BLOCKS, LANES)], 2),
            np.stack([-st.reshape(KF, BLOCKS, LANES), ct.reshape(KF, BLOCKS, LANES)], 2),
        ],
        0,
    )
    to_columns = columns.transpose(1, 0, 2, 3).reshape(BLOCKS, PAIR, 2 * LANES)
    from_columns = to_columns.transpose(0, 2, 1)
    low, high = full[:HALO], full[HALO + N :]
    blank = np.zeros((HALO, PAIR), np.float32)
    rims = np.stack(
        [
            np.concatenate([blank, low[::-1]], 0),
            np.concatenate([blank, low], 0),
            np.concatenate([high[::-1], blank], 0),
            np.concatenate([high, blank], 0),
        ]
    )
    back = np.concatenate([cos.T, -sin.T], 0)
    back_low, back_high = back[:, :HALO], back[:, HALO + N :]
    blank = np.zeros((PAIR, HALO), np.float32)
    margins = np.stack(
        [
            np.concatenate([back_high[:, ::-1], blank], 1),
            np.concatenate([back_high, blank], 1),
            np.concatenate([blank, back_low[:, ::-1]], 1),
            np.concatenate([blank, back_low], 1),
        ]
    )
    tables = (mid, mid.T, to_columns, from_columns, rims, back[:, HALO : HALO + N], margins)
    return tuple(np.ascontiguousarray(one).astype(ml_dtypes.bfloat16) for one in tables)


def dot(a, b):
    return jnp.dot(a, b, preferred_element_type=F32)


def in_left_half(shape):
    return lax.broadcasted_iota(jnp.int32, shape, 1) < KF


def swap_halves(pair):
    return pltpu.roll(pair, KF, 1)


def call(body, name, outs, args, specs=None, grid=None, scratch=(), flops=0, moved=0):
    vmem = pl.BlockSpec(memory_space=pltpu.VMEM)
    extra = {} if grid is None else {"grid": grid}
    return pl.pallas_call(
        body,
        name=name,
        out_shape=outs,
        in_specs=specs,
        out_specs=jax.tree.map(lambda _: vmem, outs),
        scratch_shapes=list(scratch),
        compiler_params=pltpu.CompilerParams(vmem_limit_bytes=VMEM_LIMIT),
        cost_estimate=pl.CostEstimate(flops=flops, bytes_accessed=moved, transcendentals=0),
        **extra,
    )(*args)


def edges_body(
    mask, mid_t, real, imag, weight, flags, up, down, side, strips, table, pair, scalar, marks, sems
):
    copies = [
        pltpu.make_async_copy(mid_t, table, sems.at[0]),
        pltpu.make_async_copy(mask.at[:, N - LANES :], strips.at[:, :LANES], sems.at[1]),
        pltpu.make_async_copy(mask.at[:, :LANES], strips.at[:, LANES:], sems.at[2]),
        pltpu.make_async_copy(real.at[0], pair.at[0], sems.at[3]),
        pltpu.make_async_copy(imag.at[0], pair.at[1], sems.at[4]),
        pltpu.make_async_copy(weight, scalar, sems.at[5]),
        pltpu.make_async_copy(flags, marks, sems.at[6]),
    ]
    for copy in copies:
        copy.start()
    for copy in copies[3:]:
        copy.wait()
    scale = jnp.sqrt(jnp.full((KF, KF), 2.0 * scalar[0], F32)) * (1.0 / (NE * KF))
    kernel = jnp.concatenate([pair[0] * scale, pair[1] * scale], 1).astype(BF16)
    row = lax.broadcasted_iota(jnp.int32, (16, LANES), 0)
    sides = jnp.where(row == 0, marks[0, 0].astype(F32), marks[0, 1].astype(F32)).astype(BF16)
    side[...] = kernel
    for out in (up, down):
        out[EDGE : EDGE + KF, :] = kernel
        out[EDGE + KF :, :] = sides
    for copy in copies[:3]:
        copy.wait()
    both = dot(table[...], strips[...]).astype(BF16)
    up[:EDGE, :] = both[:, :LANES]
    down[:EDGE, :] = both[:, LANES:]


def middle_body(mask, mid, mid_t, out):
    rows = dot(mask[...], mid[...]).astype(BF16)
    part = dot(mid_t[...], rows)

    @pl.when(pl.program_id(0) == 0)
    def _():
        out[...] = part

    @pl.when(pl.program_id(0) > 0)
    def _():
        out[...] += part


def split_kernel(pair):
    left = in_left_half(pair.shape)
    other = swap_halves(pair)
    return jnp.where(left, pair, other), jnp.where(left, other, pair)


def fields_body(count, row_count, *refs):
    (flags, middle, target, mid, to_columns, from_columns, rims, own) = refs[:8]
    packs = refs[8 : 8 + count - 1]
    out, a_ref, e_ref, v_ref, u_ref = refs[8 + count - 1 :]
    tile = lax.axis_index("tile")
    tiles = lax.axis_size("tile")
    left = in_left_half((KF, PAIR))
    blocks = middle[...]
    low = jnp.where(flags[0, 0] == 1, rims[1], rims[0])
    low = jnp.where(tile == 0, jnp.zeros_like(low), low)
    high = jnp.where(flags[0, 1] == 1, rims[3], rims[2])
    high = jnp.where(tile == tiles - 1, jnp.zeros_like(high), high)
    blocks = blocks + dot(packs[0][:EDGE, :], low) + dot(packs[1][:EDGE, :], high)
    top, bottom = blocks[:KF], swap_halves(blocks[KF:])
    spectrum = jnp.where(left, top - bottom, -(top + bottom))
    turned = swap_halves(spectrum)
    turned = jnp.where(left, -turned, turned)
    kernels = [own[...].astype(F32)]
    for index, pack in enumerate(packs):
        start = EDGE if index < 2 else 0
        kernels.append(pack[start : start + KF, :].astype(F32))
    kernels = [split_kernel(one) for one in kernels]
    begin = pl.multiple_of(lax.axis_index("kern") * row_count, row_count)
    rows = mid[pl.ds(begin, row_count), :]
    for index, (real, imag) in enumerate(kernels):
        product = real * spectrum + imag * turned
        other = swap_halves(product)
        other = jnp.where(left, -other, other)
        stacked = jnp.concatenate([product, other], 0).astype(BF16)
        a_ref[index * row_count : (index + 1) * row_count, :] = dot(rows, stacked).astype(BF16)
    step = 32 if row_count % 32 == 0 else 16
    for block in range(BLOCKS):
        e_ref[...] = dot(a_ref[...], to_columns[block])
        for r in range(0, row_count, step):
            total = None
            parts = []
            for index in range(count):
                at = index * row_count + r
                real = e_ref[at : at + step, :LANES]
                imag = e_ref[at : at + step, LANES:]
                term = real * real + imag * imag
                total = term if total is None else total + term
            wanted = target[r : r + step, block * LANES : (block + 1) * LANES].astype(F32)
            bend = jnp.tanh(total - 2.0)
            slope = (bend + (1.0 - 2.0 * wanted)) * (1.0 - bend * bend)
            for index in range(count):
                at = index * row_count + r
                v_ref[at : at + step, :LANES] = (e_ref[at : at + step, :LANES] * slope).astype(BF16)
                v_ref[at : at + step, LANES:] = (e_ref[at : at + step, LANES:] * slope).astype(BF16)
        part = dot(v_ref[...], from_columns[block])
        if block == 0:
            u_ref[...] = part
        else:
            u_ref[...] += part
    wide = jnp.concatenate(
        [u_ref[i * row_count : (i + 1) * row_count, :].astype(BF16) for i in range(count)], 1
    )
    waves = lax.dot_general(rows, wide, (((0,), (0,)), ((), ())), preferred_element_type=F32)
    total = None
    for index, (real, imag) in enumerate(kernels):
        wave = waves[:, index * PAIR : (index + 1) * PAIR]
        top, bottom = wave[:KF], swap_halves(wave[KF:])
        wave = jnp.where(left, top + bottom, top - bottom)
        other = swap_halves(wave)
        other = jnp.where(left, other, -other)
        term = real * wave + imag * other
        total = term if total is None else total + term
    for index in range(count):
        out[index] = total.astype(BF16)


def sum_body(count, parts, out):
    total = parts[0].astype(F32)
    for index in range(1, count):
        total = total + parts[index].astype(F32)
    out[...] = total.astype(BF16)


def gradient_body(row_count, own, below, above, mark_below, mark_above, mid, back, margins, out):
    left = in_left_half((KF, PAIR))
    begin = pl.multiple_of(lax.axis_index("kern") * row_count, row_count)
    rows = mid[pl.ds(begin, row_count), :]
    waves = []
    for ref in (own, below, above):
        pair = ref[...].astype(F32)
        other = swap_halves(pair)
        other = jnp.where(left, -other, other)
        waves.append(dot(rows, jnp.concatenate([pair, other], 0).astype(BF16)).astype(BF16))
    low_mark = mark_below[EDGE + KF + 1 : EDGE + KF + 2, :].astype(F32)
    high_mark = mark_above[EDGE + KF : EDGE + KF + 1, :].astype(F32)
    low = jnp.where(low_mark == 1.0, margins[1].astype(F32), margins[0].astype(F32)).astype(BF16)
    high = jnp.where(high_mark == 1.0, margins[3].astype(F32), margins[2].astype(F32)).astype(BF16)
    out[:, :LANES] = dot(waves[0], back[:, :LANES]) + dot(waves[1], low)
    out[:, LANES : N - LANES] = dot(waves[0], back[:, LANES : N - LANES])
    out[:, N - LANES :] = dot(waves[0], back[:, N - LANES :]) + dot(waves[2], high)


def per_device(mask_pixels, orientation, target_pattern, kernel_real, kernel_imag, eigen_weights):
    tables = tuple(jnp.asarray(one) for one in transform_tables())
    mid, mid_t, to_columns, from_columns, rims, back, margins = tables
    tiles, count = lax.axis_size("tile"), lax.axis_size("kern")
    row_count = target_pattern.shape[0]
    vmem = pl.BlockSpec(memory_space=pltpu.VMEM)
    smem = pl.BlockSpec(memory_space=pltpu.SMEM)
    packed = jax.ShapeDtypeStruct((PACK, LANES), BF16)
    small = jax.ShapeDtypeStruct((KF, PAIR), BF16)

    up, down, side = call(
        edges_body,
        "edges",
        (packed, packed, small),
        (mask_pixels, mid_t, kernel_real, kernel_imag, eigen_weights, orientation),
        [pl.BlockSpec(memory_space=pltpu.HBM)] * 6,
        scratch=[
            pltpu.VMEM((N, 2 * LANES), BF16),
            pltpu.VMEM((PAIR, N), BF16),
            pltpu.VMEM((2, KF, KF), F32),
            pltpu.SMEM((1,), F32),
            pltpu.SMEM((1, 2), jnp.int32),
            pltpu.SemaphoreType.DMA((7,)),
        ],
        flops=2 * N * LANES * PAIR * 2,
        moved=N * LANES * 4,
    )

    def shifted(tile_step, kern_step):
        pairs = []
        for t in range(tiles):
            for k in range(count):
                there = ((t + tile_step) % tiles) * count + (k - kern_step) % count
                pairs.append((t * count + k, there))
        return pairs

    packs = []
    for kern_step in range(1, count):
        if kern_step <= 2:
            value, tile_step = ((up, 1), (down, -1))[kern_step - 1]
        else:
            value, tile_step = side, 0
        packs.append(lax.ppermute(value, ("tile", "kern"), shifted(tile_step, kern_step)))

    chunk = 384
    middle = call(
        middle_body,
        "middle",
        jax.ShapeDtypeStruct((PAIR, PAIR), F32),
        (mask_pixels, mid, mid_t),
        [
            pl.BlockSpec((chunk, N), lambda i: (i, 0)),
            vmem,
            pl.BlockSpec((PAIR, chunk), lambda i: (0, i)),
        ],
        grid=(N // chunk,),
        flops=4 * N * N * PAIR,
        moved=N * N * 2,
    )

    part = call(
        functools.partial(fields_body, count, row_count),
        "fields",
        jax.ShapeDtypeStruct((count, KF, PAIR), BF16),
        (orientation, middle, target_pattern, mid, to_columns, from_columns, rims, side, *packs),
        [smem] + [vmem] * (7 + count - 1),
        scratch=[
            pltpu.VMEM((count * row_count, PAIR), BF16),
            pltpu.VMEM((count * row_count, 2 * LANES), F32),
            pltpu.VMEM((count * row_count, 2 * LANES), BF16),
            pltpu.VMEM((count * row_count, PAIR), F32),
        ],
        flops=8 * count * row_count * N * PAIR,
        moved=4 * row_count * N,
    )

    parts = lax.all_to_all(part, "kern", 0, 0)
    own = call(functools.partial(sum_body, count), "total", small, (parts,), [vmem])
    forward = [(i, i + 1) for i in range(tiles - 1)]
    below = lax.ppermute(own, "tile", forward)
    above = lax.ppermute(own, "tile", [(target, source) for source, target in forward])
    return call(
        functools.partial(gradient_body, row_count),
        "gradient",
        jax.ShapeDtypeStruct((row_count, N), F32),
        (own, below, above, packs[0], packs[1], mid, back, margins),
        [vmem] * 8,
        flops=2 * row_count * PAIR * (N + 5 * PAIR),
        moved=4 * row_count * N,
    )


def solution(mesh):
    in_specs = (
        P(None, "tile"),
        P("tile", None),
        P("kern", "tile"),
        P("kern", None, None),
        P("kern", None, None),
        P("kern"),
    )
    out_specs = P("kern", "tile")
    return jax.shard_map(
        per_device, mesh=mesh, in_specs=in_specs, out_specs=out_specs, check_vma=False
    )
```

profile of v0, /device:TPU:4, one launch (start us, length us, event | category | flops | bytes accessed | tf_op | source)
XLA Modules:
  0.0 41.2 jit_solution(3735000064063137303)
XLA Ops:
  0.7 0.0 copy-start
  0.7 1.7 %copy-done = bf16[1152,1152]{1,0:T(8,128)(2,1)S(1)} copy-done((bf16[1152,1152]{1,0:T(8,128)(2,1)S(1)}, bf16[1152,1152]{1,0:T(8,128)(2,1)}, u32[]{:S(2)}) %copy-start) | copy-done | bytes 2654232
  2.4 1.0 %copy-done.2 = bf16[128,1152]{1,0:T(8,128)(2,1)S(1)} copy-done((bf16[128,1152]{1,0:T(8,128)(2,1)S(1)}, bf16[128,1152]{1,0:T(8,128)(2,1)}, u32[]{:S(2)}) %copy-start.2) | copy-done | bytes 294936
  3.4 0.8 %copy-done.5 = f32[1,64,64]{2,1,0:T(8,128)S(1)} copy-done((f32[1,64,64]{2,1,0:T(8,128)S(1)}, f32[1,64,64]{2,1,0:T(8,128)}, u32[]{:S(2)}) %copy-start.5) | copy-done | bytes 16408
  4.1 0.8 %copy-done.6 = f32[1,64,64]{2,1,0:T(8,128)S(1)} copy-done((f32[1,64,64]{2,1,0:T(8,128)S(1)}, f32[1,64,64]{2,1,0:T(8,128)}, u32[]{:S(2)}) %copy-start.6) | copy-done | bytes 16408
  4.9 0.7 %copy-done.7 = s32[1,2]{1,0:T(1,128)S(1)} copy-done((s32[1,2]{1,0:T(1,128)S(1)}, s32[1,2]{1,0:T(1,128)}, u32[]{:S(2)}) %copy-start.7) | copy-done | bytes 32
  5.5 1.2 %edges.1 = (bf16[208,128]{1,0:T(8,128)(2,1)S(1)}, bf16[208,128]{1,0:T(8,128)(2,1)S(1)}, bf16[64,128]{1,0:T(8,128)(2,1)S(1)}) custom-call(bf16[1152,1152]{1,0:T(8,128)(2,1)S(1)} %copy-done, bf16[128,1152]{1,0:T(8,128)(2,1)S(1)} %copy-done.2, f32[1,64,64]{2,1,0:T(8,128)S(1)} %copy-done.5, f32[1,64,64]{2,1,0:T(8,128)S(1)} %copy-done.6, f32[1]{0:T(128)S(6)} %copy.14.weight, ...), custom_call_target="tpu_custom_call" | custom-call | flops 75497472 | bytes 589824 | tf_op jit(solution)/shard_map/edges/pallas_call | solution.py:88
  6.8 1.6 %collective-permute-start.2 = (bf16[64,128]{1,0:T(8,128)(2,1)S(1)}, bf16[64,128]{1,0:T(8,128)(2,1)S(1)}, u32[]{:S(2)}, u32[]{:S(2)}) collective-permute-start(bf16[64,128]{1,0:T(8,128)(2,1)S(1)} %get-tuple-element.8.refs_7_), channel_id=1, source_target_pairs={{0,1},{1,2},{2,3},{3,0},{4,5},{5,6},{6,7},{7,4},{8,9},{9,10},{10,1... | collective-permute-start | bytes 49160 | tf_op jit(solution)/shard_map/ppermute | solution.py:290
  8.4 1.5 %collective-permute-start = (bf16[208,128]{1,0:T(8,128)(2,1)S(1)}, bf16[208,128]{1,0:T(8,128)(2,1)S(1)}, u32[]{:S(2)}, u32[]{:S(2)}) collective-permute-start(bf16[208,128]{1,0:T(8,128)(2,1)S(1)} %get-tuple-element.9), channel_id=1, source_target_pairs={{0,7},{1,4},{2,5},{3,6},{4,11},{5,8},{6,9},{7,10},{8,15},{9,12},{1... | collective-permute-start | bytes 159752 | tf_op jit(solution)/shard_map/ppermute | solution.py:290
  9.9 0.0 copy-start.12
  9.9 3.1 %collective-permute-start.1 = (bf16[208,128]{1,0:T(8,128)(2,1)S(1)}, bf16[208,128]{1,0:T(8,128)(2,1)S(1)}, u32[]{:S(2)}, u32[]{:S(2)}) collective-permute-start(bf16[208,128]{1,0:T(8,128)(2,1)S(1)} %get-tuple-element.10), channel_id=1, source_target_pairs={{0,30},{1,31},{2,28},{3,29},{4,2},{5,3},{6,0},{7,1},{8,6},{9,7},{1... | collective-permute-start | bytes 159752 | tf_op jit(solution)/shard_map/ppermute | solution.py:290
  13.0 0.0 copy-done.1
  13.0 1.8 %middle.1.refs_1_ = f32[128,128]{1,0:T(8,128)S(1)} custom-call(bf16[1152,1152]{1,0:T(8,128)(2,1)S(1)} %copy-done, bf16[1152,128]{1,0:T(8,128)(2,1)S(1)} %copy-done.1, bf16[128,1152]{1,0:T(8,128)(2,1)S(1)} %copy-done.2), custom_call_target="tpu_custom_call" | custom-call | flops 679477248 | bytes 2654208 | tf_op jit(solution)/shard_map/middle/pallas_call | solution.py:88
  14.8 0.0 copy-start.3
  14.8 0.0 copy-start.4
  14.8 0.0 collective-permute-done.2.refs_10_
  14.9 0.0 collective-permute-done.refs_8_.mark_below
  14.9 0.0 collective-permute-done.1.refs_9_.mark_above
  14.9 0.0 copy-done.8
  14.9 0.0 copy-done.9
  14.9 0.0 copy-done.10
  14.9 0.0 copy-done.11
  14.9 0.0 copy-done.12
  14.9 4.9 %fields.1 = bf16[4,64,128]{2,1,0:T(8,128)(2,1)S(1)} custom-call(s32[1,2]{1,0:T(1,128)S(1)} %copy-done.8, f32[128,128]{1,0:T(8,128)S(1)} %middle.1.refs_1_, s32[288,1152]{1,0:T(8,128)S(1)} %copy-done.9, bf16[1152,128]{1,0:T(8,128)(2,1)S(1)} %copy-done.1, bf16[9,128,256]{2,1,0:T(8,128)(2,1)S(1)} %copy-done.11, bf16[9,256,128]{2,1,0:T(8,128)(2,1)S(1)} %copy-done.10, ...), custom_call_target="tpu_custom_call" | custom-call | flops 1358954496 | bytes 1327104 | tf_op jit(solution)/shard_map/fields/pallas_call | solution.py:88
  19.9 9.8 %all_to_all.5.parts = bf16[4,64,128]{2,1,0:T(8,128)(2,1)S(1)} all-to-all(bf16[4,64,128]{2,1,0:T(8,128)(2,1)S(1)} %fields.1), channel_id=1, replica_groups=mesh['tile'=8,'kern'=4] {'kern'}, dimensions={0} | all-to-all | bytes 131072 | tf_op jit(solution)/shard_map/all_to_all | solution.py:324
  29.7 3.9 %collective-permute-start.4 = (bf16[64,128]{1,0:T(8,128)(2,1)S(1)}, bf16[64,128]{1,0:T(8,128)(2,1)S(1)}, u32[]{:S(2)}, u32[]{:S(2)}) collective-permute-start(bf16[64,128]{1,0:T(8,128)(2,1)S(1)} %total.1.own), channel_id=1, source_target_pairs={{4,0},{8,4},{12,8},{16,12},{20,16},{24,20},{28,24},{5,1},{9,5},{13... | collective-permute-start | bytes 49160 | tf_op jit(solution)/shard_map/ppermute | solution.py:328
  33.6 1.9 %collective-permute-start.3 = (bf16[64,128]{1,0:T(8,128)(2,1)S(1)}, bf16[64,128]{1,0:T(8,128)(2,1)S(1)}, u32[]{:S(2)}, u32[]{:S(2)}) collective-permute-start(bf16[64,128]{1,0:T(8,128)(2,1)S(1)} %total.1.own), channel_id=1, source_target_pairs={{0,4},{4,8},{8,12},{12,16},{16,20},{20,24},{24,28},{1,5},{5,9},{9,... | collective-permute-start | bytes 49160 | tf_op jit(solution)/shard_map/ppermute | solution.py:327
  35.5 0.0 collective-permute-done.4.above
  35.5 4.0 %collective-permute-done.3.below = bf16[64,128]{1,0:T(8,128)(2,1)S(1)} collective-permute-done((bf16[64,128]{1,0:T(8,128)(2,1)S(1)}, bf16[64,128]{1,0:T(8,128)(2,1)S(1)}, u32[]{:S(2)}, u32[]{:S(2)}) %collective-permute-start.3) | collective-permute-done | bytes 16416 | tf_op jit(solution)/shard_map/ppermute | solution.py:327
  39.6 0.0 copy-done.3
  39.6 0.0 copy-done.4
  39.6 1.6 %gradient.1 = f32[288,1152]{1,0:T(8,128)} custom-call(bf16[64,128]{1,0:T(8,128)(2,1)S(1)} %total.1.own, bf16[64,128]{1,0:T(8,128)(2,1)S(1)} %collective-permute-done.3.below, bf16[64,128]{1,0:T(8,128)(2,1)S(1)} %collective-permute-done.4.above, bf16[208,128]{1,0:T(8,128)(2,1)S(1)} %collective-permute-done.refs_8_.mark_below, ...), custom_call_target="tpu_custom_call" | custom-call | flops 132120576 | bytes 1327104 | tf_op jit(solution)/shard_map/gradient/pallas_call | solution.py:88
  (10 shorter events, 0.0 us)
Async XLA Ops:
  0.7 1.8 %copy-start = (bf16[1152,1152]{1,0:T(8,128)(2,1)S(1)}, bf16[1152,1152]{1,0:T(8,128)(2,1)}, u32[]{:S(2)}) copy-start(bf16[1152,1152]{1,0:T(8,128)(2,1)} %mask.3) | copy-start | bytes 7962628
  2.4 1.0 %copy-start.2 = (bf16[128,1152]{1,0:T(8,128)(2,1)S(1)}, bf16[128,1152]{1,0:T(8,128)(2,1)}, u32[]{:S(2)}) copy-start(bf16[128,1152]{1,0:T(8,128)(2,1)} %constant.15.clone.mid_t) | copy-start | bytes 884740
  3.4 0.8 %copy-start.5 = (f32[1,64,64]{2,1,0:T(8,128)S(1)}, f32[1,64,64]{2,1,0:T(8,128)}, u32[]{:S(2)}) copy-start(f32[1,64,64]{2,1,0:T(8,128)} %real.1) | copy-start | bytes 49156
  4.1 0.8 %copy-start.6 = (f32[1,64,64]{2,1,0:T(8,128)S(1)}, f32[1,64,64]{2,1,0:T(8,128)}, u32[]{:S(2)}) copy-start(f32[1,64,64]{2,1,0:T(8,128)} %imag.1) | copy-start | bytes 49156
  4.9 0.7 %copy-start.7 = (s32[1,2]{1,0:T(1,128)S(1)}, s32[1,2]{1,0:T(1,128)}, u32[]{:S(2)}) copy-start(s32[1,2]{1,0:T(1,128)} %refs_0_.1) | copy-start | bytes 28
  5.5 7.5 %copy-start.1 = (bf16[1152,128]{1,0:T(8,128)(2,1)S(1)}, bf16[1152,128]{1,0:T(8,128)(2,1)}, u32[]{:S(2)}) copy-start(bf16[1152,128]{1,0:T(8,128)(2,1)} %constant.14.clone.mid.refs_3_) | copy-start | bytes 884740
  6.8 8.1 %collective-permute-start.2 = (bf16[64,128]{1,0:T(8,128)(2,1)S(1)}, bf16[64,128]{1,0:T(8,128)(2,1)S(1)}, u32[]{:S(2)}, u32[]{:S(2)}) collective-permute-start(bf16[64,128]{1,0:T(8,128)(2,1)S(1)} %get-tuple-element.8.refs_7_), channel_id=1, source_target_pairs={{0,1},{1,2},{2,3},{3,0},{4,5},{5,6},{6,7},{7,4},{8,9},{9,10},{10,1... | collective-permute-start | bytes 49160 | tf_op jit(solution)/shard_map/ppermute | solution.py:290
  8.4 6.5 %collective-permute-start = (bf16[208,128]{1,0:T(8,128)(2,1)S(1)}, bf16[208,128]{1,0:T(8,128)(2,1)S(1)}, u32[]{:S(2)}, u32[]{:S(2)}) collective-permute-start(bf16[208,128]{1,0:T(8,128)(2,1)S(1)} %get-tuple-element.9), channel_id=1, source_target_pairs={{0,7},{1,4},{2,5},{3,6},{4,11},{5,8},{6,9},{7,10},{8,15},{9,12},{1... | collective-permute-start | bytes 159752 | tf_op jit(solution)/shard_map/ppermute | solution.py:290
  9.9 5.0 %copy-start.8 = (s32[1,2]{1,0:T(1,128)S(1)}, s32[1,2]{1,0:T(1,128)}, u32[]{:S(2)}) copy-start(s32[1,2]{1,0:T(1,128)} %refs_0_.1) | copy-start | bytes 28
  9.9 5.0 %copy-start.9 = (s32[288,1152]{1,0:T(8,128)S(1)}, s32[288,1152]{1,0:T(8,128)}, u32[]{:S(2)}) copy-start(s32[288,1152]{1,0:T(8,128)} %refs_2_.1) | copy-start | bytes 3981316
  9.9 5.0 %copy-start.10 = (bf16[9,256,128]{2,1,0:T(8,128)(2,1)S(1)}, bf16[9,256,128]{2,1,0:T(8,128)(2,1)}, u32[]{:S(2)}) copy-start(bf16[9,256,128]{2,1,0:T(8,128)(2,1)} %constant.17.clone.refs_5_) | copy-start | bytes 1769476
  9.9 5.0 %copy-start.11 = (bf16[9,128,256]{2,1,0:T(8,128)(2,1)S(1)}, bf16[9,128,256]{2,1,0:T(8,128)(2,1)}, u32[]{:S(2)}) copy-start(bf16[9,128,256]{2,1,0:T(8,128)(2,1)} %constant.16.clone.refs_4_) | copy-start | bytes 1769476
  9.9 5.0 %copy-start.12 = (bf16[4,128,128]{2,1,0:T(8,128)(2,1)S(1)}, bf16[4,128,128]{2,1,0:T(8,128)(2,1)}, u32[]{:S(2)}) copy-start(bf16[4,128,128]{2,1,0:T(8,128)(2,1)} %constant.18.clone.refs_6_) | copy-start | bytes 393220
  9.9 4.9 %collective-permute-start.1 = (bf16[208,128]{1,0:T(8,128)(2,1)S(1)}, bf16[208,128]{1,0:T(8,128)(2,1)S(1)}, u32[]{:S(2)}, u32[]{:S(2)}) collective-permute-start(bf16[208,128]{1,0:T(8,128)(2,1)S(1)} %get-tuple-element.10), channel_id=1, source_target_pairs={{0,30},{1,31},{2,28},{3,29},{4,2},{5,3},{6,0},{7,1},{8,6},{9,7},{1... | collective-permute-start | bytes 159752 | tf_op jit(solution)/shard_map/ppermute | solution.py:290
  14.8 24.7 %copy-start.3 = (bf16[128,1152]{1,0:T(8,128)(2,1)S(1)}, bf16[128,1152]{1,0:T(8,128)(2,1)}, u32[]{:S(2)}) copy-start(bf16[128,1152]{1,0:T(8,128)(2,1)} %constant.19.clone.back) | copy-start | bytes 884740
  14.8 24.7 %copy-start.4 = (bf16[4,128,128]{2,1,0:T(8,128)(2,1)S(1)}, bf16[4,128,128]{2,1,0:T(8,128)(2,1)}, u32[]{:S(2)}) copy-start(bf16[4,128,128]{2,1,0:T(8,128)(2,1)} %constant.20.clone.margins) | copy-start | bytes 393220
  29.7 5.9 %collective-permute-start.4 = (bf16[64,128]{1,0:T(8,128)(2,1)S(1)}, bf16[64,128]{1,0:T(8,128)(2,1)S(1)}, u32[]{:S(2)}, u32[]{:S(2)}) collective-permute-start(bf16[64,128]{1,0:T(8,128)(2,1)S(1)} %total.1.own), channel_id=1, source_target_pairs={{4,0},{8,4},{12,8},{16,12},{20,16},{24,20},{28,24},{5,1},{9,5},{13... | collective-permute-start | bytes 49160 | tf_op jit(solution)/shard_map/ppermute | solution.py:328
  33.6 6.0 %collective-permute-start.3 = (bf16[64,128]{1,0:T(8,128)(2,1)S(1)}, bf16[64,128]{1,0:T(8,128)(2,1)S(1)}, u32[]{:S(2)}, u32[]{:S(2)}) collective-permute-start(bf16[64,128]{1,0:T(8,128)(2,1)S(1)} %total.1.own), channel_id=1, source_target_pairs={{0,4},{4,8},{8,12},{12,16},{16,20},{20,24},{24,28},{1,5},{5,9},{9,... | collective-permute-start | bytes 49160 | tf_op jit(solution)/shard_map/ppermute | solution.py:327
where the time goes:
time: 41.6 us; the launch traced here: 41.2 us
  starting transfers between devices  12.1 us (29%)
  blocking collectives  9.79 us (24%)
  Pallas kernels  9.57 us (23%)
  local copies, waits for them, and re-layouts  4.91 us (12%)
  waiting for transfers between devices  4.03 us (10%)
  between operations  0.81 us (2%)
    all_to_all x1, blocking collectives, per_device(): parts = lax.all_to_all(part, 'kern', 0, 0)  9.79 us
    pallas_call x5, Pallas kernels, call(): pl.pallas_call(body, name=name, out_shape=outs, in_specs=specs, out_specs...  9.57 us
    ppermute x3, starting transfers between devices, per_device(): lax.ppermute(value, ('tile', 'kern'), shifted(tile_step, kern_step))  6.24 us
    unnamed x26, local copies, waits for them, and re-layouts  4.91 us
    ppermute x1, waiting for transfers between devices, per_device(): below = lax.ppermute(own, 'tile', forward)  4.02 us
    ppermute x1, starting transfers between devices, per_device(): lax.ppermute(own, 'tile', [(target, source) for source, target in forward])  3.92 us
    ppermute x1, starting transfers between devices, per_device(): below = lax.ppermute(own, 'tile', forward)  1.92 us
  transfers between devices with their start and end apart: 5, of which 1 were waited for; matrix products, arithmetic and copies ran while one was open for 0% of the time, Pallas kernels for 4%

commit v1 on v0

--- a/solution.py
+++ b/solution.py
@@ -22,6 +22,8 @@
 BF16 = jnp.bfloat16
 F32 = jnp.float32
 VMEM_LIMIT = 32 * 1024 * 1024
+EDGES_LIMIT = 62 * 1024 * 1024
+MIDDLE_LIMIT = 61 * 1024 * 1024
 
 
 def wave_tables():
@@ -82,7 +84,15 @@
     return pltpu.roll(pair, KF, 1)
 
 
-def call(body, name, outs, args, specs=None, grid=None, scratch=(), flops=0, moved=0):
+def kern_steps(count):
+    return (1, 3, 2) if count == 4 else range(1, count)
+
+
+def destination(k, step, count):
+    return k ^ step if count == 4 else (k - step) % count
+
+
+def call(body, name, outs, args, specs=None, grid=None, scratch=(), flops=0, moved=0, vmem_bytes=VMEM_LIMIT):
     vmem = pl.BlockSpec(memory_space=pltpu.VMEM)
     extra = {} if grid is None else {"grid": grid}
     return pl.pallas_call(
@@ -92,19 +102,22 @@
         in_specs=specs,
         out_specs=jax.tree.map(lambda _: vmem, outs),
         scratch_shapes=list(scratch),
-        compiler_params=pltpu.CompilerParams(vmem_limit_bytes=VMEM_LIMIT),
+        compiler_params=pltpu.CompilerParams(vmem_limit_bytes=vmem_bytes),
         cost_estimate=pl.CostEstimate(flops=flops, bytes_accessed=moved, transcendentals=0),
         **extra,
     )(*args)
 
 
 def edges_body(
-    mask, mid_t, real, imag, weight, flags, up, down, side, strips, table, pair, scalar, marks, sems
+    mask, mid_t, real, imag, weight, flags, mate, other, side, strips, table, pair, scalar, marks, sems
 ):
+    odd = lax.rem(lax.axis_index("tile"), 2)
+    facing = pl.multiple_of((1 - odd) * (N - LANES), LANES)
+    facing_other = pl.multiple_of(odd * (N - LANES), LANES)
     copies = [
         pltpu.make_async_copy(mid_t, table, sems.at[0]),
-        pltpu.make_async_copy(mask.at[:, N - LANES :], strips.at[:, :LANES], sems.at[1]),
-        pltpu.make_async_copy(mask.at[:, :LANES], strips.at[:, LANES:], sems.at[2]),
+        pltpu.make_async_copy(mask.at[:, pl.ds(facing, LANES)], strips.at[:, :LANES], sems.at[1]),
+        pltpu.make_async_copy(mask.at[:, pl.ds(facing_other, LANES)], strips.at[:, LANES:], sems.at[2]),
         pltpu.make_async_copy(real.at[0], pair.at[0], sems.at[3]),
         pltpu.make_async_copy(imag.at[0], pair.at[1], sems.at[4]),
         pltpu.make_async_copy(weight, scalar, sems.at[5]),
@@ -119,14 +132,14 @@
     row = lax.broadcasted_iota(jnp.int32, (16, LANES), 0)
     sides = jnp.where(row == 0, marks[0, 0].astype(F32), marks[0, 1].astype(F32)).astype(BF16)
     side[...] = kernel
-    for out in (up, down):
+    for out in (mate, other):
         out[EDGE : EDGE + KF, :] = kernel
         out[EDGE + KF :, :] = sides
     for copy in copies[:3]:
         copy.wait()
     both = dot(table[...], strips[...]).astype(BF16)
-    up[:EDGE, :] = both[:, :LANES]
-    down[:EDGE, :] = both[:, LANES:]
+    mate[:EDGE, :] = both[:, :LANES]
+    other[:EDGE, :] = both[:, LANES:]
 
 
 def middle_body(mask, mid, mid_t, out):
@@ -160,7 +173,9 @@
     low = jnp.where(tile == 0, jnp.zeros_like(low), low)
     high = jnp.where(flags[0, 1] == 1, rims[3], rims[2])
     high = jnp.where(tile == tiles - 1, jnp.zeros_like(high), high)
-    blocks = blocks + dot(packs[0][:EDGE, :], low) + dot(packs[1][:EDGE, :], high)
+    odd = lax.rem(tile, 2) == 1
+    low, high = jnp.where(odd, low, high), jnp.where(odd, high, low)
+    blocks = blocks + dot(packs[1][:EDGE, :], low) + dot(packs[0][:EDGE, :], high)
     top, bottom = blocks[:KF], swap_halves(blocks[KF:])
     spectrum = jnp.where(left, top - bottom, -(top + bottom))
     turned = swap_halves(spectrum)
@@ -179,15 +194,17 @@
         stacked = jnp.concatenate([product, other], 0).astype(BF16)
         a_ref[index * row_count : (index + 1) * row_count, :] = dot(rows, stacked).astype(BF16)
     step = 32 if row_count % 32 == 0 else 16
+    e_ref[0] = dot(a_ref[...], to_columns[0])
     for block in range(BLOCKS):
-        e_ref[...] = dot(a_ref[...], to_columns[block])
+        now = block % 2
+        if block + 1 < BLOCKS:
+            e_ref[1 - now] = dot(a_ref[...], to_columns[block + 1])
         for r in range(0, row_count, step):
             total = None
-            parts = []
             for index in range(count):
                 at = index * row_count + r
-                real = e_ref[at : at + step, :LANES]
-                imag = e_ref[at : at + step, LANES:]
+                real = e_ref[now, at : at + step, :LANES]
+                imag = e_ref[now, at : at + step, LANES:]
                 term = real * real + imag * imag
                 total = term if total is None else total + term
             wanted = target[r : r + step, block * LANES : (block + 1) * LANES].astype(F32)
@@ -195,9 +212,10 @@
             slope = (bend + (1.0 - 2.0 * wanted)) * (1.0 - bend * bend)
             for index in range(count):
                 at = index * row_count + r
-                v_ref[at : at + step, :LANES] = (e_ref[at : at + step, :LANES] * slope).astype(BF16)
-                v_ref[at : at + step, LANES:] = (e_ref[at : at + step, LANES:] * slope).astype(BF16)
-        part = dot(v_ref[...], from_columns[block])
+                for half in (slice(0, LANES), slice(LANES, 2 * LANES)):
+                    field = e_ref[now, at : at + step, half]
+                    v_ref[now, at : at + step, half] = (field * slope).astype(BF16)
+        part = dot(v_ref[now], from_columns[block])
         if block == 0:
             u_ref[...] = part
         else:
@@ -215,34 +233,37 @@
         other = jnp.where(left, other, -other)
         term = real * wave + imag * other
         total = term if total is None else total + term
-    for index in range(count):
-        out[index] = total.astype(BF16)
-
-
-def sum_body(count, parts, out):
-    total = parts[0].astype(F32)
-    for index in range(1, count):
-        total = total + parts[index].astype(F32)
     out[...] = total.astype(BF16)
 
 
-def gradient_body(row_count, own, below, above, mark_below, mark_above, mid, back, margins, out):
+def sum_body(count, *refs):
+    total = refs[0][...].astype(F32)
+    for one in refs[1:count]:
+        total = total + one[...].astype(F32)
+    refs[count][...] = total.astype(BF16)
+
+
+def gradient_body(row_count, own, near, far, near_pack, far_pack, mid, back, margins, out):
     left = in_left_half((KF, PAIR))
     begin = pl.multiple_of(lax.axis_index("kern") * row_count, row_count)
     rows = mid[pl.ds(begin, row_count), :]
     waves = []
-    for ref in (own, below, above):
+    for ref in (own, near, far):
         pair = ref[...].astype(F32)
         other = swap_halves(pair)
         other = jnp.where(left, -other, other)
         waves.append(dot(rows, jnp.concatenate([pair, other], 0).astype(BF16)).astype(BF16))
-    low_mark = mark_below[EDGE + KF + 1 : EDGE + KF + 2, :].astype(F32)
-    high_mark = mark_above[EDGE + KF : EDGE + KF + 1, :].astype(F32)
+    odd = lax.rem(lax.axis_index("tile"), 2) == 1
+    below, above = jnp.where(odd, waves[1], waves[2]), jnp.where(odd, waves[2], waves[1])
+    near_marks = near_pack[EDGE + KF :, :].astype(F32)
+    far_marks = far_pack[EDGE + KF :, :].astype(F32)
+    low_mark = jnp.where(odd, near_marks, far_marks)[1:2]
+    high_mark = jnp.where(odd, far_marks, near_marks)[0:1]
     low = jnp.where(low_mark == 1.0, margins[1].astype(F32), margins[0].astype(F32)).astype(BF16)
     high = jnp.where(high_mark == 1.0, margins[3].astype(F32), margins[2].astype(F32)).astype(BF16)
-    out[:, :LANES] = dot(waves[0], back[:, :LANES]) + dot(waves[1], low)
+    out[:, :LANES] = dot(waves[0], back[:, :LANES]) + dot(below, low)
     out[:, LANES : N - LANES] = dot(waves[0], back[:, LANES : N - LANES])
-    out[:, N - LANES :] = dot(waves[0], back[:, N - LANES :]) + dot(waves[2], high)
+    out[:, N - LANES :] = dot(waves[0], back[:, N - LANES :]) + dot(above, high)
 
 
 def per_device(mask_pixels, orientation, target_pattern, kernel_real, kernel_imag, eigen_weights):
@@ -255,7 +276,7 @@
     packed = jax.ShapeDtypeStruct((PACK, LANES), BF16)
     small = jax.ShapeDtypeStruct((KF, PAIR), BF16)
 
-    up, down, side = call(
+    mate, other, side = call(
         edges_body,
         "edges",
         (packed, packed, small),
@@ -271,23 +292,28 @@
         ],
         flops=2 * N * LANES * PAIR * 2,
         moved=N * LANES * 4,
-    )
-
-    def shifted(tile_step, kern_step):
+        vmem_bytes=EDGES_LIMIT,
+    )
+
+    def swapped(move_tile, step):
         pairs = []
         for t in range(tiles):
             for k in range(count):
-                there = ((t + tile_step) % tiles) * count + (k - kern_step) % count
-                pairs.append((t * count + k, there))
+                pairs.append((t * count + k, move_tile(t) * count + destination(k, step, count)))
         return pairs
 
+    def chip_mate(t):
+        return t ^ 1
+
+    def other_side(t):
+        return (t + 1 if t % 2 else t - 1) % tiles
+
     packs = []
-    for kern_step in range(1, count):
-        if kern_step <= 2:
-            value, tile_step = ((up, 1), (down, -1))[kern_step - 1]
-        else:
-            value, tile_step = side, 0
-        packs.append(lax.ppermute(value, ("tile", "kern"), shifted(tile_step, kern_step)))
+    for step in kern_steps(count):
+        value, move_tile = {0: (other, other_side), 1: (mate, chip_mate)}.get(
+            len(packs), (side, lambda t: t)
+        )
+        packs.append(lax.ppermute(value, ("tile", "kern"), swapped(move_tile, step)))
 
     chunk = 384
     middle = call(
@@ -303,34 +329,38 @@
         grid=(N // chunk,),
         flops=4 * N * N * PAIR,
         moved=N * N * 2,
+        vmem_bytes=MIDDLE_LIMIT,
     )
 
     part = call(
         functools.partial(fields_body, count, row_count),
         "fields",
-        jax.ShapeDtypeStruct((count, KF, PAIR), BF16),
+        small,
         (orientation, middle, target_pattern, mid, to_columns, from_columns, rims, side, *packs),
         [smem] + [vmem] * (7 + count - 1),
         scratch=[
             pltpu.VMEM((count * row_count, PAIR), BF16),
-            pltpu.VMEM((count * row_count, 2 * LANES), F32),
-            pltpu.VMEM((count * row_count, 2 * LANES), BF16),
+            pltpu.VMEM((2, count * row_count, 2 * LANES), F32),
+            pltpu.VMEM((2, count * row_count, 2 * LANES), BF16),
             pltpu.VMEM((count * row_count, PAIR), F32),
         ],
         flops=8 * count * row_count * N * PAIR,
         moved=4 * row_count * N,
     )
 
-    parts = lax.all_to_all(part, "kern", 0, 0)
-    own = call(functools.partial(sum_body, count), "total", small, (parts,), [vmem])
-    forward = [(i, i + 1) for i in range(tiles - 1)]
-    below = lax.ppermute(own, "tile", forward)
-    above = lax.ppermute(own, "tile", [(target, source) for source, target in forward])
+    parts = [part]
+    for step in kern_steps(count):
+        pairs = [(k, destination(k, step, count)) for k in range(count)]
+        parts.append(lax.ppermute(part, "kern", pairs))
+    own = call(functools.partial(sum_body, count), "total", small, tuple(parts), [vmem] * count)
+    near = lax.ppermute(own, "tile", [(t, chip_mate(t)) for t in range(tiles)])
+    inner = [t for t in range(tiles) if 0 < t < tiles - 1]
+    far = lax.ppermute(own, "tile", [(t, other_side(t)) for t in inner])
     return call(
         functools.partial(gradient_body, row_count),
         "gradient",
         jax.ShapeDtypeStruct((row_count, N), F32),
-        (own, below, above, packs[0], packs[1], mid, back, margins),
+        (own, near, far, packs[1], packs[0], mid, back, margins),
         [vmem] * 8,
         flops=2 * row_count * PAIR * (N + 5 * PAIR),
         moved=4 * row_count * N,

time: 41.6 us -> 33.4 us (0.80)
  blocking collectives: 9.79 us -> 0 us
  local copies, waits for them, and re-layouts: 4.91 us -> 0.88 us
  Pallas kernels: 9.57 us -> 12.9 us
  waiting for transfers between devices: 4.03 us -> 7.13 us
  starting transfers between devices: 12.1 us -> 11.6 us
    all_to_all x1 -> x0, blocking collectives: 9.79 us -> none  [per_device(): parts = lax.all_to_all(part, 'kern', 0, 0)]
    unnamed x26 -> x20, local copies, waits for them, and re-layouts: 4.91 us -> 0.88 us
    pallas_call x5, Pallas kernels: 9.57 us -> 12.9 us  [call(): pl.pallas_call(body, name=name, out_shape=outs, in_specs=specs, out_specs...]
    ppermute x5 -> x8, waiting for transfers between devices: 4.03 us -> 7.13 us  [the longest x1 3.38 us: per_device(): far = lax.ppermute(own, 'tile', [(t, other_side(t)) for t in inner])]
    ppermute x5 -> x8, starting transfers between devices: 12.1 us -> 11.6 us  [the longest x3 5.17 us: per_device(): lax.ppermute(value, ('tile', 'kern'), swapped(move_tile, step))]
  transfers between devices with their start and end apart: 5 -> 8, of which waited for: 1 -> 5; matrix products, arithmetic and copies ran while one was open for 0% -> 0% of each run, Pallas kernels for 4% -> 13%
where the time goes in v1:
time: 33.4 us; the launch traced here: 33.2 us
  Pallas kernels  12.9 us (39%)
  starting transfers between devices  11.6 us (35%)
  waiting for transfers between devices  7.13 us (21%)
  local copies, waits for them, and re-layouts  0.88 us (3%)
  between operations  0.77 us (2%)
    pallas_call x5, Pallas kernels, call(): pl.pallas_call(body, name=name, out_shape=outs, in_specs=specs, out_specs...  12.9 us
    ppermute x3, starting transfers between devices, per_device(): lax.ppermute(value, ('tile', 'kern'), swapped(move_tile, step))  5.17 us
    ppermute x3, starting transfers between devices, per_device(): parts.append(lax.ppermute(part, 'kern', pairs))  3.82 us
    ppermute x1, waiting for transfers between devices, per_device(): far = lax.ppermute(own, 'tile', [(t, other_side(t)) for t in inner])  3.38 us
    ppermute x3, waiting for transfers between devices, per_device(): parts.append(lax.ppermute(part, 'kern', pairs))  3.25 us
    ppermute x1, starting transfers between devices, per_device(): far = lax.ppermute(own, 'tile', [(t, other_side(t)) for t in inner])  1.92 us
    unnamed x20, local copies, waits for them, and re-layouts  0.88 us
  transfers between devices with their start and end apart: 8, of which 5 were waited for; matrix products, arithmetic and copies ran while one was open for 0% of the time, Pallas kernels for 13%

profile of v1, /device:TPU:4, one launch (start us, length us, event | category | flops | bytes accessed | tf_op | source)
XLA Modules:
  0.0 33.2 jit_solution(10903163643376611206)
XLA Ops:
  0.7 2.2 %edges.1 = (bf16[208,128]{1,0:T(8,128)(2,1)}, bf16[208,128]{1,0:T(8,128)(2,1)}, bf16[64,128]{1,0:T(8,128)(2,1)}) custom-call(bf16[1152,1152]{1,0:T(8,128)(2,1)} %mask.3, bf16[128,1152]{1,0:T(8,128)(2,1)} %constant.15.clone.mid_t, f32[1,64,64]{2,1,0:T(8,128)} %real.1, f32[1,64,64]{2,1,0:T(8,128)} %imag.1, f32[1]{0:T(128)S(6)} %copy.14.weight, s32[1,2]{1,0:T(1,128)} %refs_0_.1), custom_call_target="tpu_custom_call" | custom-call | flops 75497472 | bytes 589824 | tf_op jit(solution)/shard_map/edges/pallas_call | solution.py:98
  2.8 2.7 %collective-permute-start.2 = (bf16[64,128]{1,0:T(8,128)(2,1)}, bf16[64,128]{1,0:T(8,128)(2,1)S(1)}, u32[]{:S(2)}, u32[]{:S(2)}) collective-permute-start(bf16[64,128]{1,0:T(8,128)(2,1)} %get-tuple-element.8.refs_7_), channel_id=1, source_target_pairs={{0,2},{1,3},{2,0},{3,1},{4,6},{5,7},{6,4},{7,5},{8,10},{9,11},{10,... | collective-permute-start | bytes 49160 | tf_op jit(solution)/shard_map/ppermute | solution.py:316
  5.5 1.6 %collective-permute-start = (bf16[208,128]{1,0:T(8,128)(2,1)}, bf16[208,128]{1,0:T(8,128)(2,1)S(1)}, u32[]{:S(2)}, u32[]{:S(2)}) collective-permute-start(bf16[208,128]{1,0:T(8,128)(2,1)} %get-tuple-element.9), channel_id=1, source_target_pairs={{0,29},{1,28},{2,31},{3,30},{4,9},{5,8},{6,11},{7,10},{8,5},{9,4},... | collective-permute-start | bytes 159752 | tf_op jit(solution)/shard_map/ppermute | solution.py:316
  7.1 0.0 copy-start.7
  7.1 0.0 copy-start.8
  7.1 0.0 copy-start.9
  7.1 0.9 %collective-permute-start.1 = (bf16[208,128]{1,0:T(8,128)(2,1)}, bf16[208,128]{1,0:T(8,128)(2,1)S(1)}, u32[]{:S(2)}, u32[]{:S(2)}) collective-permute-start(bf16[208,128]{1,0:T(8,128)(2,1)} %get-tuple-element.10), channel_id=1, source_target_pairs={{0,7},{1,6},{2,5},{3,4},{4,3},{5,2},{6,1},{7,0},{8,15},{9,14},{10,... | collective-permute-start | bytes 159752 | tf_op jit(solution)/shard_map/ppermute | solution.py:316
  8.0 4.2 %middle.1.refs_1_ = f32[128,128]{1,0:T(8,128)} custom-call(bf16[1152,1152]{1,0:T(8,128)(2,1)} %mask.3, bf16[1152,128]{1,0:T(8,128)(2,1)} %constant.14.clone.mid.refs_3_, bf16[128,1152]{1,0:T(8,128)(2,1)} %constant.15.clone.mid_t), custom_call_target="tpu_custom_call" | custom-call | flops 679477248 | bytes 2654208 | tf_op jit(solution)/shard_map/middle/pallas_call | solution.py:98
  12.3 0.0 collective-permute-done.2.refs_10_
  12.3 0.0 collective-permute-done.refs_8_.far_pack
  12.3 0.5 %collective-permute-done.1.refs_9_.near_pack = bf16[208,128]{1,0:T(8,128)(2,1)S(1)} collective-permute-done((bf16[208,128]{1,0:T(8,128)(2,1)}, bf16[208,128]{1,0:T(8,128)(2,1)S(1)}, u32[]{:S(2)}, u32[]{:S(2)}) %collective-permute-start.1) | collective-permute-done | bytes 53280 | tf_op jit(solution)/shard_map/ppermute | solution.py:316
  12.8 0.0 copy-done
  12.8 0.0 copy-done.4
  12.8 0.0 copy-done.5
  12.8 0.0 copy-done.6
  12.8 0.0 copy-done.7
  12.8 0.0 copy-done.8
  12.8 0.0 copy-start.3
  12.8 0.8 %copy-done.3 = f32[128,128]{1,0:T(8,128)S(1)} copy-done((f32[128,128]{1,0:T(8,128)S(1)}, f32[128,128]{1,0:T(8,128)}, u32[]{:S(2)}) %copy-start.3) | copy-done | bytes 65560
  13.7 4.9 %fields.1.refs_0_ = bf16[64,128]{1,0:T(8,128)(2,1)S(1)} custom-call(s32[1,2]{1,0:T(1,128)S(1)} %copy-done.4, f32[128,128]{1,0:T(8,128)S(1)} %copy-done.3, s32[288,1152]{1,0:T(8,128)S(1)} %copy-done.5, bf16[1152,128]{1,0:T(8,128)(2,1)S(1)} %copy-done, bf16[9,128,256]{2,1,0:T(8,128)(2,1)S(1)} %copy-done.8, bf16[9,256,128]{2,1,0:T(8,128)(2,1)S(1)} %copy-done.7, ...), custom_call_target="tpu_custom_call" | custom-call | flops 1358954496 | bytes 1327104 | tf_op jit(solution)/shard_map/fields/pallas_call | solution.py:98
  18.5 1.3 %collective-permute-start.5 = (bf16[64,128]{1,0:T(8,128)(2,1)S(1)}, bf16[64,128]{1,0:T(8,128)(2,1)S(1)}, u32[]{:S(2)}, u32[]{:S(2)}) collective-permute-start(bf16[64,128]{1,0:T(8,128)(2,1)S(1)} %fields.1.refs_0_), channel_id=1, source_target_pairs={{0,2},{1,3},{2,0},{3,1},{4,6},{5,7},{6,4},{7,5},{8,10},{9,11},{10,... | collective-permute-start | bytes 49160 | tf_op jit(solution)/shard_map/ppermute | solution.py:354
  19.9 2.0 %collective-permute-start.4 = (bf16[64,128]{1,0:T(8,128)(2,1)S(1)}, bf16[64,128]{1,0:T(8,128)(2,1)S(1)}, u32[]{:S(2)}, u32[]{:S(2)}) collective-permute-start(bf16[64,128]{1,0:T(8,128)(2,1)S(1)} %fields.1.refs_0_), channel_id=1, source_target_pairs={{0,3},{1,2},{2,1},{3,0},{4,7},{5,6},{6,5},{7,4},{8,11},{9,10},{10,... | collective-permute-start | bytes 49160 | tf_op jit(solution)/shard_map/ppermute | solution.py:354
  21.8 0.5 %collective-permute-start.3 = (bf16[64,128]{1,0:T(8,128)(2,1)S(1)}, bf16[64,128]{1,0:T(8,128)(2,1)S(1)}, u32[]{:S(2)}, u32[]{:S(2)}) collective-permute-start(bf16[64,128]{1,0:T(8,128)(2,1)S(1)} %fields.1.refs_0_), channel_id=1, source_target_pairs={{0,1},{1,0},{2,3},{3,2},{4,5},{5,4},{6,7},{7,6},{8,9},{9,8},{10,11... | collective-permute-start | bytes 49160 | tf_op jit(solution)/shard_map/ppermute | solution.py:354
  22.3 1.0 %collective-permute-done.5.refs_3_ = bf16[64,128]{1,0:T(8,128)(2,1)S(1)} collective-permute-done((bf16[64,128]{1,0:T(8,128)(2,1)S(1)}, bf16[64,128]{1,0:T(8,128)(2,1)S(1)}, u32[]{:S(2)}, u32[]{:S(2)}) %collective-permute-start.5) | collective-permute-done | bytes 16416 | tf_op jit(solution)/shard_map/ppermute | solution.py:354
  23.4 2.0 %collective-permute-done.4.refs_2_ = bf16[64,128]{1,0:T(8,128)(2,1)S(1)} collective-permute-done((bf16[64,128]{1,0:T(8,128)(2,1)S(1)}, bf16[64,128]{1,0:T(8,128)(2,1)S(1)}, u32[]{:S(2)}, u32[]{:S(2)}) %collective-permute-start.4) | collective-permute-done | bytes 16416 | tf_op jit(solution)/shard_map/ppermute | solution.py:354
  25.4 0.2 collective-permute-done.3.refs_1_
  25.6 1.9 %collective-permute-start.7 = (bf16[64,128]{1,0:T(8,128)(2,1)S(1)}, bf16[64,128]{1,0:T(8,128)(2,1)S(1)}, u32[]{:S(2)}, u32[]{:S(2)}) collective-permute-start(bf16[64,128]{1,0:T(8,128)(2,1)S(1)} %total.1.own), channel_id=1, source_target_pairs={{4,8},{8,4},{12,16},{16,12},{20,24},{24,20},{5,9},{9,5},{13,17},{1... | collective-permute-start | bytes 49160 | tf_op jit(solution)/shard_map/ppermute | solution.py:358
  27.5 0.6 %collective-permute-start.6 = (bf16[64,128]{1,0:T(8,128)(2,1)S(1)}, bf16[64,128]{1,0:T(8,128)(2,1)S(1)}, u32[]{:S(2)}, u32[]{:S(2)}) collective-permute-start(bf16[64,128]{1,0:T(8,128)(2,1)S(1)} %total.1.own), channel_id=1, source_target_pairs={{0,4},{4,0},{8,12},{12,8},{16,20},{20,16},{24,28},{28,24},{1,5},{5... | collective-permute-start | bytes 49160 | tf_op jit(solution)/shard_map/ppermute | solution.py:356
  28.2 3.4 %collective-permute-done.7.far = bf16[64,128]{1,0:T(8,128)(2,1)S(1)} collective-permute-done((bf16[64,128]{1,0:T(8,128)(2,1)S(1)}, bf16[64,128]{1,0:T(8,128)(2,1)S(1)}, u32[]{:S(2)}, u32[]{:S(2)}) %collective-permute-start.7) | collective-permute-done | bytes 16416 | tf_op jit(solution)/shard_map/ppermute | solution.py:358
  31.6 0.0 collective-permute-done.6.near
  31.6 0.0 copy-done.1
  31.6 1.6 %gradient.1 = f32[288,1152]{1,0:T(8,128)} custom-call(bf16[64,128]{1,0:T(8,128)(2,1)S(1)} %total.1.own, bf16[64,128]{1,0:T(8,128)(2,1)S(1)} %collective-permute-done.6.near, bf16[64,128]{1,0:T(8,128)(2,1)S(1)} %collective-permute-done.7.far, bf16[208,128]{1,0:T(8,128)(2,1)S(1)} %collective-permute-done.1.refs_9_.near_pack, ...), custom_call_target="tpu_custom_call" | custom-call | flops 132120576 | bytes 1327104 | tf_op jit(solution)/shard_map/gradient/pallas_call | solution.py:98
  (9 shorter events, 0.0 us)
Async XLA Ops:
  2.8 9.4 %collective-permute-start.2 = (bf16[64,128]{1,0:T(8,128)(2,1)}, bf16[64,128]{1,0:T(8,128)(2,1)S(1)}, u32[]{:S(2)}, u32[]{:S(2)}) collective-permute-start(bf16[64,128]{1,0:T(8,128)(2,1)} %get-tuple-element.8.refs_7_), channel_id=1, source_target_pairs={{0,2},{1,3},{2,0},{3,1},{4,6},{5,7},{6,4},{7,5},{8,10},{9,11},{10,... | collective-permute-start | bytes 49160 | tf_op jit(solution)/shard_map/ppermute | solution.py:316
  5.5 6.8 %collective-permute-start = (bf16[208,128]{1,0:T(8,128)(2,1)}, bf16[208,128]{1,0:T(8,128)(2,1)S(1)}, u32[]{:S(2)}, u32[]{:S(2)}) collective-permute-start(bf16[208,128]{1,0:T(8,128)(2,1)} %get-tuple-element.9), channel_id=1, source_target_pairs={{0,29},{1,28},{2,31},{3,30},{4,9},{5,8},{6,11},{7,10},{8,5},{9,4},... | collective-permute-start | bytes 159752 | tf_op jit(solution)/shard_map/ppermute | solution.py:316
  7.1 5.7 %copy-start = (bf16[1152,128]{1,0:T(8,128)(2,1)S(1)}, bf16[1152,128]{1,0:T(8,128)(2,1)}, u32[]{:S(2)}) copy-start(bf16[1152,128]{1,0:T(8,128)(2,1)} %constant.14.clone.mid.refs_3_) | copy-start | bytes 884740
  7.1 5.7 %copy-start.4 = (s32[1,2]{1,0:T(1,128)S(1)}, s32[1,2]{1,0:T(1,128)}, u32[]{:S(2)}) copy-start(s32[1,2]{1,0:T(1,128)} %refs_0_.1) | copy-start | bytes 28
  7.1 5.7 %copy-start.5 = (s32[288,1152]{1,0:T(8,128)S(1)}, s32[288,1152]{1,0:T(8,128)}, u32[]{:S(2)}) copy-start(s32[288,1152]{1,0:T(8,128)} %refs_2_.1) | copy-start | bytes 3981316
  7.1 5.7 %copy-start.6 = (bf16[64,128]{1,0:T(8,128)(2,1)S(1)}, bf16[64,128]{1,0:T(8,128)(2,1)}, u32[]{:S(2)}) copy-start(bf16[64,128]{1,0:T(8,128)(2,1)} %get-tuple-element.8.refs_7_) | copy-start | bytes 49156
  7.1 5.7 %copy-start.7 = (bf16[9,256,128]{2,1,0:T(8,128)(2,1)S(1)}, bf16[9,256,128]{2,1,0:T(8,128)(2,1)}, u32[]{:S(2)}) copy-start(bf16[9,256,128]{2,1,0:T(8,128)(2,1)} %constant.17.clone.refs_5_) | copy-start | bytes 1769476
  7.1 5.7 %copy-start.8 = (bf16[9,128,256]{2,1,0:T(8,128)(2,1)S(1)}, bf16[9,128,256]{2,1,0:T(8,128)(2,1)}, u32[]{:S(2)}) copy-start(bf16[9,128,256]{2,1,0:T(8,128)(2,1)} %constant.16.clone.refs_4_) | copy-start | bytes 1769476
  7.1 5.7 %copy-start.9 = (bf16[4,128,128]{2,1,0:T(8,128)(2,1)S(1)}, bf16[4,128,128]{2,1,0:T(8,128)(2,1)}, u32[]{:S(2)}) copy-start(bf16[4,128,128]{2,1,0:T(8,128)(2,1)} %constant.18.clone.refs_6_) | copy-start | bytes 393220
  7.1 5.6 %collective-permute-start.1 = (bf16[208,128]{1,0:T(8,128)(2,1)}, bf16[208,128]{1,0:T(8,128)(2,1)S(1)}, u32[]{:S(2)}, u32[]{:S(2)}) collective-permute-start(bf16[208,128]{1,0:T(8,128)(2,1)} %get-tuple-element.10), channel_id=1, source_target_pairs={{0,7},{1,6},{2,5},{3,4},{4,3},{5,2},{6,1},{7,0},{8,15},{9,14},{10,... | collective-permute-start | bytes 159752 | tf_op jit(solution)/shard_map/ppermute | solution.py:316
  12.2 19.3 %copy-start.1 = (bf16[128,1152]{1,0:T(8,128)(2,1)S(1)}, bf16[128,1152]{1,0:T(8,128)(2,1)}, u32[]{:S(2)}) copy-start(bf16[128,1152]{1,0:T(8,128)(2,1)} %constant.19.clone.back) | copy-start | bytes 884740
  12.3 19.3 %copy-start.2 = (bf16[4,128,128]{2,1,0:T(8,128)(2,1)S(1)}, bf16[4,128,128]{2,1,0:T(8,128)(2,1)}, u32[]{:S(2)}) copy-start(bf16[4,128,128]{2,1,0:T(8,128)(2,1)} %constant.20.clone.margins) | copy-start | bytes 393220
  12.8 0.8 %copy-start.3 = (f32[128,128]{1,0:T(8,128)S(1)}, f32[128,128]{1,0:T(8,128)}, u32[]{:S(2)}) copy-start(f32[128,128]{1,0:T(8,128)} %middle.1.refs_1_) | copy-start | bytes 196612
  18.5 4.8 %collective-permute-start.5 = (bf16[64,128]{1,0:T(8,128)(2,1)S(1)}, bf16[64,128]{1,0:T(8,128)(2,1)S(1)}, u32[]{:S(2)}, u32[]{:S(2)}) collective-permute-start(bf16[64,128]{1,0:T(8,128)(2,1)S(1)} %fields.1.refs_0_), channel_id=1, source_target_pairs={{0,2},{1,3},{2,0},{3,1},{4,6},{5,7},{6,4},{7,5},{8,10},{9,11},{10,... | collective-permute-start | bytes 49160 | tf_op jit(solution)/shard_map/ppermute | solution.py:354
  19.9 5.5 %collective-permute-start.4 = (bf16[64,128]{1,0:T(8,128)(2,1)S(1)}, bf16[64,128]{1,0:T(8,128)(2,1)S(1)}, u32[]{:S(2)}, u32[]{:S(2)}) collective-permute-start(bf16[64,128]{1,0:T(8,128)(2,1)S(1)} %fields.1.refs_0_), channel_id=1, source_target_pairs={{0,3},{1,2},{2,1},{3,0},{4,7},{5,6},{6,5},{7,4},{8,11},{9,10},{10,... | collective-permute-start | bytes 49160 | tf_op jit(solution)/shard_map/ppermute | solution.py:354
  21.8 3.7 %collective-permute-start.3 = (bf16[64,128]{1,0:T(8,128)(2,1)S(1)}, bf16[64,128]{1,0:T(8,128)(2,1)S(1)}, u32[]{:S(2)}, u32[]{:S(2)}) collective-permute-start(bf16[64,128]{1,0:T(8,128)(2,1)S(1)} %fields.1.refs_0_), channel_id=1, source_target_pairs={{0,1},{1,0},{2,3},{3,2},{4,5},{5,4},{6,7},{7,6},{8,9},{9,8},{10,11... | collective-permute-start | bytes 49160 | tf_op jit(solution)/shard_map/ppermute | solution.py:354
  25.6 6.0 %collective-permute-start.7 = (bf16[64,128]{1,0:T(8,128)(2,1)S(1)}, bf16[64,128]{1,0:T(8,128)(2,1)S(1)}, u32[]{:S(2)}, u32[]{:S(2)}) collective-permute-start(bf16[64,128]{1,0:T(8,128)(2,1)S(1)} %total.1.own), channel_id=1, source_target_pairs={{4,8},{8,4},{12,16},{16,12},{20,24},{24,20},{5,9},{9,5},{13,17},{1... | collective-permute-start | bytes 49160 | tf_op jit(solution)/shard_map/ppermute | solution.py:358
  27.5 4.0 %collective-permute-start.6 = (bf16[64,128]{1,0:T(8,128)(2,1)S(1)}, bf16[64,128]{1,0:T(8,128)(2,1)S(1)}, u32[]{:S(2)}, u32[]{:S(2)}) collective-permute-start(bf16[64,128]{1,0:T(8,128)(2,1)S(1)} %total.1.own), channel_id=1, source_target_pairs={{0,4},{4,0},{8,12},{12,8},{16,20},{20,16},{24,28},{28,24},{1,5},{5... | collective-permute-start | bytes 49160 | tf_op jit(solution)/shard_map/ppermute | solution.py:356

commit v2 on v1

--- a/solution.py
+++ b/solution.py
@@ -22,8 +22,6 @@
 BF16 = jnp.bfloat16
 F32 = jnp.float32
 VMEM_LIMIT = 32 * 1024 * 1024
-EDGES_LIMIT = 62 * 1024 * 1024
-MIDDLE_LIMIT = 61 * 1024 * 1024
 
 
 def wave_tables():
@@ -109,25 +107,28 @@
 
 
 def edges_body(
-    mask, mid_t, real, imag, weight, flags, mate, other, side, strips, table, pair, scalar, marks, sems
+    mask, mid, mid_t, real, imag, weight, flags, mate, other, side, held, tall, table, pair, marks, sems
 ):
-    odd = lax.rem(lax.axis_index("tile"), 2)
-    facing = pl.multiple_of((1 - odd) * (N - LANES), LANES)
-    facing_other = pl.multiple_of(odd * (N - LANES), LANES)
+    odd = lax.rem(lax.axis_index("tile"), 2) == 1
     copies = [
         pltpu.make_async_copy(mid_t, table, sems.at[0]),
-        pltpu.make_async_copy(mask.at[:, pl.ds(facing, LANES)], strips.at[:, :LANES], sems.at[1]),
-        pltpu.make_async_copy(mask.at[:, pl.ds(facing_other, LANES)], strips.at[:, LANES:], sems.at[2]),
+        pltpu.make_async_copy(mask.at[:, :LANES], held.at[:, :LANES], sems.at[1]),
+        pltpu.make_async_copy(mask.at[:, N - LANES :], held.at[:, N - LANES :], sems.at[2]),
         pltpu.make_async_copy(real.at[0], pair.at[0], sems.at[3]),
         pltpu.make_async_copy(imag.at[0], pair.at[1], sems.at[4]),
-        pltpu.make_async_copy(weight, scalar, sems.at[5]),
-        pltpu.make_async_copy(flags, marks, sems.at[6]),
+        pltpu.make_async_copy(flags, marks, sems.at[5]),
     ]
+    inner = pltpu.make_async_copy(
+        mask.at[:, LANES : N - LANES], held.at[:, LANES : N - LANES], sems.at[6]
+    )
+    columns = pltpu.make_async_copy(mid, tall, sems.at[7])
     for copy in copies:
         copy.start()
+    inner.start()
+    columns.start()
     for copy in copies[3:]:
         copy.wait()
-    scale = jnp.sqrt(jnp.full((KF, KF), 2.0 * scalar[0], F32)) * (1.0 / (NE * KF))
+    scale = jnp.sqrt(jnp.full((KF, KF), 2.0 * weight[0], F32)) * (1.0 / (NE * KF))
     kernel = jnp.concatenate([pair[0] * scale, pair[1] * scale], 1).astype(BF16)
     row = lax.broadcasted_iota(jnp.int32, (16, LANES), 0)
     sides = jnp.where(row == 0, marks[0, 0].astype(F32), marks[0, 1].astype(F32)).astype(BF16)
@@ -137,22 +138,17 @@
         out[EDGE + KF :, :] = sides
     for copy in copies[:3]:
         copy.wait()
-    both = dot(table[...], strips[...]).astype(BF16)
-    mate[:EDGE, :] = both[:, :LANES]
-    other[:EDGE, :] = both[:, LANES:]
+    strips = jnp.concatenate([held[:, :LANES], held[:, N - LANES :]], 1)
+    both = dot(table[...], strips)
+    first, last = both[:, :LANES], both[:, LANES:]
+    mate[:EDGE, :] = jnp.where(odd, first, last).astype(BF16)
+    other[:EDGE, :] = jnp.where(odd, last, first).astype(BF16)
+    inner.wait()
+    columns.wait()
 
 
 def middle_body(mask, mid, mid_t, out):
-    rows = dot(mask[...], mid[...]).astype(BF16)
-    part = dot(mid_t[...], rows)
-
-    @pl.when(pl.program_id(0) == 0)
-    def _():
-        out[...] = part
-
-    @pl.when(pl.program_id(0) > 0)
-    def _():
-        out[...] += part
+    out[...] = dot(mid_t[...], dot(mask[...], mid[...]).astype(BF16))
 
 
 def split_kernel(pair):
@@ -266,6 +262,10 @@
     out[:, N - LANES :] = dot(waves[0], back[:, N - LANES :]) + dot(above, high)
 
 
+def far_off(array):
+    return pltpu.with_memory_space_constraint(array, pltpu.HBM)
+
+
 def per_device(mask_pixels, orientation, target_pattern, kernel_real, kernel_imag, eigen_weights):
     tables = tuple(jnp.asarray(one) for one in transform_tables())
     mid, mid_t, to_columns, from_columns, rims, back, margins = tables
@@ -273,26 +273,34 @@
     row_count = target_pattern.shape[0]
     vmem = pl.BlockSpec(memory_space=pltpu.VMEM)
     smem = pl.BlockSpec(memory_space=pltpu.SMEM)
+    hbm = pl.BlockSpec(memory_space=pltpu.HBM)
     packed = jax.ShapeDtypeStruct((PACK, LANES), BF16)
     small = jax.ShapeDtypeStruct((KF, PAIR), BF16)
 
-    mate, other, side = call(
+    mate, other, side, held, mid, mid_t = call(
         edges_body,
         "edges",
-        (packed, packed, small),
-        (mask_pixels, mid_t, kernel_real, kernel_imag, eigen_weights, orientation),
-        [pl.BlockSpec(memory_space=pltpu.HBM)] * 6,
+        (
+            pltpu.VMEM((PACK, LANES), BF16),
+            pltpu.VMEM((PACK, LANES), BF16),
+            pltpu.VMEM((KF, PAIR), BF16),
+            pltpu.VMEM((N, N), BF16),
+            pltpu.VMEM((N, PAIR), BF16),
+            pltpu.VMEM((PAIR, N), BF16),
+        ),
+        (
+            *(far_off(one) for one in (mask_pixels, mid, mid_t, kernel_real, kernel_imag)),
+            eigen_weights,
+            far_off(orientation),
+        ),
+        [hbm] * 5 + [smem, hbm],
         scratch=[
-            pltpu.VMEM((N, 2 * LANES), BF16),
-            pltpu.VMEM((PAIR, N), BF16),
             pltpu.VMEM((2, KF, KF), F32),
-            pltpu.SMEM((1,), F32),
             pltpu.SMEM((1, 2), jnp.int32),
-            pltpu.SemaphoreType.DMA((7,)),
+            pltpu.SemaphoreType.DMA((8,)),
         ],
         flops=2 * N * LANES * PAIR * 2,
         moved=N * LANES * 4,
-        vmem_bytes=EDGES_LIMIT,
     )
 
     def swapped(move_tile, step):
@@ -315,21 +323,14 @@
         )
         packs.append(lax.ppermute(value, ("tile", "kern"), swapped(move_tile, step)))
 
-    chunk = 384
     middle = call(
         middle_body,
         "middle",
         jax.ShapeDtypeStruct((PAIR, PAIR), F32),
-        (mask_pixels, mid, mid_t),
-        [
-            pl.BlockSpec((chunk, N), lambda i: (i, 0)),
-            vmem,
-            pl.BlockSpec((PAIR, chunk), lambda i: (0, i)),
-        ],
-        grid=(N // chunk,),
+        (held, mid, mid_t),
+        [vmem] * 3,
         flops=4 * N * N * PAIR,
         moved=N * N * 2,
-        vmem_bytes=MIDDLE_LIMIT,
     )
 
     part = call(

time: 33.4 us -> 31.4 us (0.940)
  Pallas kernels: 12.9 us -> 9.71 us
  waiting for transfers between devices: 7.13 us -> 8.94 us
  local copies, waits for them, and re-layouts: 0.88 us -> 0.04 us
    pallas_call x5, Pallas kernels: 12.9 us -> 9.71 us  [call(): pl.pallas_call(body, name=name, out_shape=outs, in_specs=specs, out_specs...]
    ppermute x3, waiting for transfers between devices: 0.5 us -> 3.4 us  [per_device(): lax.ppermute(value, ('tile', 'kern'), swapped(move_tile, step))]
    unnamed x20 -> x14, local copies, waits for them, and re-layouts: 0.88 us -> 0.04 us
    ppermute x1, waiting for transfers between devices: 3.38 us -> 2.83 us  [per_device(): far = lax.ppermute(own, 'tile', [(t, other_side(t)) for t in inner])]
    ppermute x3, waiting for transfers between devices: 3.25 us -> 2.71 us  [per_device(): parts.append(lax.ppermute(part, 'kern', pairs))]
  transfers between devices with their start and end apart: 8 -> 8, of which waited for: 5 -> 6; matrix products, arithmetic and copies ran while one was open for 0% -> 0% of each run, Pallas kernels for 13% -> 3%
where the time goes in v2:
time: 31.4 us; the launch traced here: 31.2 us
  starting transfers between devices  11.8 us (38%)
  Pallas kernels  9.71 us (31%)
  waiting for transfers between devices  8.94 us (28%)
  between operations  0.79 us (3%)
    pallas_call x5, Pallas kernels, call(): pl.pallas_call(body, name=name, out_shape=outs, in_specs=specs, out_specs...  9.71 us
    ppermute x3, starting transfers between devices, per_device(): lax.ppermute(value, ('tile', 'kern'), swapped(move_tile, step))  5.1 us
    ppermute x3, starting transfers between devices, per_device(): parts.append(lax.ppermute(part, 'kern', pairs))  3.55 us
    ppermute x3, waiting for transfers between devices, per_device(): lax.ppermute(value, ('tile', 'kern'), swapped(move_tile, step))  3.4 us
    ppermute x1, waiting for transfers between devices, per_device(): far = lax.ppermute(own, 'tile', [(t, other_side(t)) for t in inner])  2.83 us
    ppermute x3, waiting for transfers between devices, per_device(): parts.append(lax.ppermute(part, 'kern', pairs))  2.71 us
    ppermute x1, starting transfers between devices, per_device(): far = lax.ppermute(own, 'tile', [(t, other_side(t)) for t in inner])  2.23 us
    ppermute x1, starting transfers between devices, per_device(): near = lax.ppermute(own, 'tile', [(t, chip_mate(t)) for t in range(tiles)])  0.89 us
  transfers between devices with their start and end apart: 8, of which 6 were waited for; matrix products, arithmetic and copies ran while one was open for 0% of the time, Pallas kernels for 3%

profile of v2, /device:TPU:4, one launch (start us, length us, event | category | flops | bytes accessed | tf_op | source)
XLA Modules:
  0.0 31.2 jit_solution(2365062290522310028)
XLA Ops:
  0.7 0.0 copy-start.2
  0.7 0.0 copy-start.3
  0.7 0.0 copy-start.4
  0.7 0.0 copy-start.5
  0.7 0.0 copy-start.6
  0.7 2.1 %edges.1 = (bf16[208,128]{1,0:T(8,128)(2,1)S(1)}, bf16[208,128]{1,0:T(8,128)(2,1)S(1)}, bf16[64,128]{1,0:T(8,128)(2,1)S(1)}, bf16[1152,1152]{1,0:T(8,128)(2,1)S(...) custom-call(bf16[1152,1152]{1,0:T(8,128)(2,1)} %mask.1, bf16[1152,128]{1,0:T(8,128)(2,1)} %constant.14.clone.mid, ...), custom_call_target="tpu_custom_call" | custom-call | flops 75497472 | bytes 589824 | tf_op jit(solution)/shard_map/edges/pallas_call | solution.py:96
  2.8 2.7 %collective-permute-start.2 = (bf16[64,128]{1,0:T(8,128)(2,1)S(1)}, bf16[64,128]{1,0:T(8,128)(2,1)S(1)}, u32[]{:S(2)}, u32[]{:S(2)}) collective-permute-start(bf16[64,128]{1,0:T(8,128)(2,1)S(1)} %get-tuple-element.14.refs_7_), channel_id=1, source_target_pairs={{0,2},{1,3},{2,0},{3,1},{4,6},{5,7},{6,4},{7,5},{8,10},{9,11},{10,... | collective-permute-start | bytes 49160 | tf_op jit(solution)/shard_map/ppermute | solution.py:324
  5.5 1.6 %collective-permute-start = (bf16[208,128]{1,0:T(8,128)(2,1)S(1)}, bf16[208,128]{1,0:T(8,128)(2,1)S(1)}, u32[]{:S(2)}, u32[]{:S(2)}) collective-permute-start(bf16[208,128]{1,0:T(8,128)(2,1)S(1)} %get-tuple-element.15), channel_id=1, source_target_pairs={{0,29},{1,28},{2,31},{3,30},{4,9},{5,8},{6,11},{7,10},{8,5},{9,4},... | collective-permute-start | bytes 159752 | tf_op jit(solution)/shard_map/ppermute | solution.py:324
  7.1 0.8 %collective-permute-start.1 = (bf16[208,128]{1,0:T(8,128)(2,1)S(1)}, bf16[208,128]{1,0:T(8,128)(2,1)S(1)}, u32[]{:S(2)}, u32[]{:S(2)}) collective-permute-start(bf16[208,128]{1,0:T(8,128)(2,1)S(1)} %get-tuple-element.16), channel_id=1, source_target_pairs={{0,7},{1,6},{2,5},{3,4},{4,3},{5,2},{6,1},{7,0},{8,15},{9,14},{10,... | collective-permute-start | bytes 159752 | tf_op jit(solution)/shard_map/ppermute | solution.py:324
  7.9 1.1 %middle.1.refs_1_ = f32[128,128]{1,0:T(8,128)S(1)} custom-call(bf16[1152,1152]{1,0:T(8,128)(2,1)S(1)} %get-tuple-element.11.mask, bf16[1152,128]{1,0:T(8,128)(2,1)S(1)} %get-tuple-element.12.mid.refs_3_, bf16[128,1152]{1,0:T(8,128)(2,1)S(1)} %get-tuple-element.13.mid_t), custom_call_target="tpu_custom_call" | custom-call | flops 679477248 | bytes 2654208 | tf_op jit(solution)/shard_map/middle/pallas_call | solution.py:96
  9.0 0.0 copy-start
  9.0 0.0 copy-start.1
  9.0 0.0 collective-permute-done.2.refs_10_
  9.1 1.8 %collective-permute-done.refs_8_.far_pack = bf16[208,128]{1,0:T(8,128)(2,1)S(1)} collective-permute-done((bf16[208,128]{1,0:T(8,128)(2,1)S(1)}, bf16[208,128]{1,0:T(8,128)(2,1)S(1)}, u32[]{:S(2)}, u32[]{:S(2)}) %collective-permute-start) | collective-permute-done | bytes 53280 | tf_op jit(solution)/shard_map/ppermute | solution.py:324
  10.8 1.6 %collective-permute-done.1.refs_9_.near_pack = bf16[208,128]{1,0:T(8,128)(2,1)S(1)} collective-permute-done((bf16[208,128]{1,0:T(8,128)(2,1)S(1)}, bf16[208,128]{1,0:T(8,128)(2,1)S(1)}, u32[]{:S(2)}, u32[]{:S(2)}) %collective-permute-start.1) | collective-permute-done | bytes 53280 | tf_op jit(solution)/shard_map/ppermute | solution.py:324
  12.5 0.0 copy-done.2
  12.5 0.0 copy-done.3
  12.5 0.0 copy-done.5
  12.5 0.0 copy-done.6
  12.5 4.9 %fields.1.refs_0_ = bf16[64,128]{1,0:T(8,128)(2,1)S(1)} custom-call(s32[1,2]{1,0:T(1,128)S(1)} %copy-done.2, f32[128,128]{1,0:T(8,128)S(1)} %middle.1.refs_1_, s32[288,1152]{1,0:T(8,128)S(1)} %copy-done.3, bf16[1152,128]{1,0:T(8,128)(2,1)S(1)} %get-tuple-element.12.mid.refs_3_, bf16[9,128,256]{2,1,0:T(8,128)(2,1)S(1)} %copy-done.5, ...), custom_call_target="tpu_custom_call" | custom-call | flops 1358954496 | bytes 1327104 | tf_op jit(solution)/shard_map/fields/pallas_call | solution.py:96
  17.4 0.1 collective-permute-start.5
  17.4 2.4 %collective-permute-start.4 = (bf16[64,128]{1,0:T(8,128)(2,1)S(1)}, bf16[64,128]{1,0:T(8,128)(2,1)S(1)}, u32[]{:S(2)}, u32[]{:S(2)}) collective-permute-start(bf16[64,128]{1,0:T(8,128)(2,1)S(1)} %fields.1.refs_0_), channel_id=1, source_target_pairs={{0,3},{1,2},{2,1},{3,0},{4,7},{5,6},{6,5},{7,4},{8,11},{9,10},{10,... | collective-permute-start | bytes 49160 | tf_op jit(solution)/shard_map/ppermute | solution.py:355
  19.9 1.0 %collective-permute-start.3 = (bf16[64,128]{1,0:T(8,128)(2,1)S(1)}, bf16[64,128]{1,0:T(8,128)(2,1)S(1)}, u32[]{:S(2)}, u32[]{:S(2)}) collective-permute-start(bf16[64,128]{1,0:T(8,128)(2,1)S(1)} %fields.1.refs_0_), channel_id=1, source_target_pairs={{0,1},{1,0},{2,3},{3,2},{4,5},{5,4},{6,7},{7,6},{8,9},{9,8},{10,11... | collective-permute-start | bytes 49160 | tf_op jit(solution)/shard_map/ppermute | solution.py:355
  20.9 1.3 %collective-permute-done.5.refs_3_ = bf16[64,128]{1,0:T(8,128)(2,1)S(1)} collective-permute-done((bf16[64,128]{1,0:T(8,128)(2,1)S(1)}, bf16[64,128]{1,0:T(8,128)(2,1)S(1)}, u32[]{:S(2)}, u32[]{:S(2)}) %collective-permute-start.5) | collective-permute-done | bytes 16416 | tf_op jit(solution)/shard_map/ppermute | solution.py:355
  22.2 1.0 %collective-permute-done.4.refs_2_ = bf16[64,128]{1,0:T(8,128)(2,1)S(1)} collective-permute-done((bf16[64,128]{1,0:T(8,128)(2,1)S(1)}, bf16[64,128]{1,0:T(8,128)(2,1)S(1)}, u32[]{:S(2)}, u32[]{:S(2)}) %collective-permute-start.4) | collective-permute-done | bytes 16416 | tf_op jit(solution)/shard_map/ppermute | solution.py:355
  23.2 0.5 %collective-permute-done.3.refs_1_ = bf16[64,128]{1,0:T(8,128)(2,1)S(1)} collective-permute-done((bf16[64,128]{1,0:T(8,128)(2,1)S(1)}, bf16[64,128]{1,0:T(8,128)(2,1)S(1)}, u32[]{:S(2)}, u32[]{:S(2)}) %collective-permute-start.3) | collective-permute-done | bytes 16416 | tf_op jit(solution)/shard_map/ppermute | solution.py:355
  23.6 2.2 %collective-permute-start.7 = (bf16[64,128]{1,0:T(8,128)(2,1)S(1)}, bf16[64,128]{1,0:T(8,128)(2,1)S(1)}, u32[]{:S(2)}, u32[]{:S(2)}) collective-permute-start(bf16[64,128]{1,0:T(8,128)(2,1)S(1)} %total.1.own), channel_id=1, source_target_pairs={{4,8},{8,4},{12,16},{16,12},{20,24},{24,20},{5,9},{9,5},{13,17},{1... | collective-permute-start | bytes 49160 | tf_op jit(solution)/shard_map/ppermute | solution.py:359
  25.9 0.9 %collective-permute-start.6 = (bf16[64,128]{1,0:T(8,128)(2,1)S(1)}, bf16[64,128]{1,0:T(8,128)(2,1)S(1)}, u32[]{:S(2)}, u32[]{:S(2)}) collective-permute-start(bf16[64,128]{1,0:T(8,128)(2,1)S(1)} %total.1.own), channel_id=1, source_target_pairs={{0,4},{4,0},{8,12},{12,8},{16,20},{20,16},{24,28},{28,24},{1,5},{5... | collective-permute-start | bytes 49160 | tf_op jit(solution)/shard_map/ppermute | solution.py:357
  26.8 2.8 %collective-permute-done.7.far = bf16[64,128]{1,0:T(8,128)(2,1)S(1)} collective-permute-done((bf16[64,128]{1,0:T(8,128)(2,1)S(1)}, bf16[64,128]{1,0:T(8,128)(2,1)S(1)}, u32[]{:S(2)}, u32[]{:S(2)}) %collective-permute-start.7) | collective-permute-done | bytes 16416 | tf_op jit(solution)/shard_map/ppermute | solution.py:359
  29.6 0.0 collective-permute-done.6.near
  29.6 0.0 copy-done
  29.6 1.6 %gradient.1 = f32[288,1152]{1,0:T(8,128)} custom-call(bf16[64,128]{1,0:T(8,128)(2,1)S(1)} %total.1.own, bf16[64,128]{1,0:T(8,128)(2,1)S(1)} %collective-permute-done.6.near, bf16[64,128]{1,0:T(8,128)(2,1)S(1)} %collective-permute-done.7.far, bf16[208,128]{1,0:T(8,128)(2,1)S(1)} %collective-permute-done.1.refs_9_.near_pack, ...), custom_call_target="tpu_custom_call" | custom-call | flops 132120576 | bytes 1327104 | tf_op jit(solution)/shard_map/gradient/pallas_call | solution.py:96
  (3 shorter events, 0.0 us)
Async XLA Ops:
  0.7 11.8 %copy-start.2 = (s32[1,2]{1,0:T(1,128)S(1)}, s32[1,2]{1,0:T(1,128)}, u32[]{:S(2)}) copy-start(s32[1,2]{1,0:T(1,128)} %refs_0_.1) | copy-start | bytes 28
  0.7 11.8 %copy-start.3 = (s32[288,1152]{1,0:T(8,128)S(1)}, s32[288,1152]{1,0:T(8,128)}, u32[]{:S(2)}) copy-start(s32[288,1152]{1,0:T(8,128)} %refs_2_.1) | copy-start | bytes 3981316
  0.7 11.8 %copy-start.4 = (bf16[9,256,128]{2,1,0:T(8,128)(2,1)S(1)}, bf16[9,256,128]{2,1,0:T(8,128)(2,1)}, u32[]{:S(2)}) copy-start(bf16[9,256,128]{2,1,0:T(8,128)(2,1)} %constant.17.clone.refs_5_) | copy-start | bytes 1769476
  0.7 11.8 %copy-start.5 = (bf16[9,128,256]{2,1,0:T(8,128)(2,1)S(1)}, bf16[9,128,256]{2,1,0:T(8,128)(2,1)}, u32[]{:S(2)}) copy-start(bf16[9,128,256]{2,1,0:T(8,128)(2,1)} %constant.16.clone.refs_4_) | copy-start | bytes 1769476
  0.7 11.8 %copy-start.6 = (bf16[4,128,128]{2,1,0:T(8,128)(2,1)S(1)}, bf16[4,128,128]{2,1,0:T(8,128)(2,1)}, u32[]{:S(2)}) copy-start(bf16[4,128,128]{2,1,0:T(8,128)(2,1)} %constant.18.clone.refs_6_) | copy-start | bytes 393220
  2.8 6.2 %collective-permute-start.2 = (bf16[64,128]{1,0:T(8,128)(2,1)S(1)}, bf16[64,128]{1,0:T(8,128)(2,1)S(1)}, u32[]{:S(2)}, u32[]{:S(2)}) collective-permute-start(bf16[64,128]{1,0:T(8,128)(2,1)S(1)} %get-tuple-element.14.refs_7_), channel_id=1, source_target_pairs={{0,2},{1,3},{2,0},{3,1},{4,6},{5,7},{6,4},{7,5},{8,10},{9,11},{10,... | collective-permute-start | bytes 49160 | tf_op jit(solution)/shard_map/ppermute | solution.py:324
  5.5 5.4 %collective-permute-start = (bf16[208,128]{1,0:T(8,128)(2,1)S(1)}, bf16[208,128]{1,0:T(8,128)(2,1)S(1)}, u32[]{:S(2)}, u32[]{:S(2)}) collective-permute-start(bf16[208,128]{1,0:T(8,128)(2,1)S(1)} %get-tuple-element.15), channel_id=1, source_target_pairs={{0,29},{1,28},{2,31},{3,30},{4,9},{5,8},{6,11},{7,10},{8,5},{9,4},... | collective-permute-start | bytes 159752 | tf_op jit(solution)/shard_map/ppermute | solution.py:324
  7.1 5.4 %collective-permute-start.1 = (bf16[208,128]{1,0:T(8,128)(2,1)S(1)}, bf16[208,128]{1,0:T(8,128)(2,1)S(1)}, u32[]{:S(2)}, u32[]{:S(2)}) collective-permute-start(bf16[208,128]{1,0:T(8,128)(2,1)S(1)} %get-tuple-element.16), channel_id=1, source_target_pairs={{0,7},{1,6},{2,5},{3,4},{4,3},{5,2},{6,1},{7,0},{8,15},{9,14},{10,... | collective-permute-start | bytes 159752 | tf_op jit(solution)/shard_map/ppermute | solution.py:324
  9.0 20.6 %copy-start = (bf16[128,1152]{1,0:T(8,128)(2,1)S(1)}, bf16[128,1152]{1,0:T(8,128)(2,1)}, u32[]{:S(2)}) copy-start(bf16[128,1152]{1,0:T(8,128)(2,1)} %constant.19.clone.back) | copy-start | bytes 884740
  9.0 20.6 %copy-start.1 = (bf16[4,128,128]{2,1,0:T(8,128)(2,1)S(1)}, bf16[4,128,128]{2,1,0:T(8,128)(2,1)}, u32[]{:S(2)}) copy-start(bf16[4,128,128]{2,1,0:T(8,128)(2,1)} %constant.20.clone.margins) | copy-start | bytes 393220
  17.4 4.8 %collective-permute-start.5 = (bf16[64,128]{1,0:T(8,128)(2,1)S(1)}, bf16[64,128]{1,0:T(8,128)(2,1)S(1)}, u32[]{:S(2)}, u32[]{:S(2)}) collective-permute-start(bf16[64,128]{1,0:T(8,128)(2,1)S(1)} %fields.1.refs_0_), channel_id=1, source_target_pairs={{0,2},{1,3},{2,0},{3,1},{4,6},{5,7},{6,4},{7,5},{8,10},{9,11},{10,... | collective-permute-start | bytes 49160 | tf_op jit(solution)/shard_map/ppermute | solution.py:355
  17.4 5.7 %collective-permute-start.4 = (bf16[64,128]{1,0:T(8,128)(2,1)S(1)}, bf16[64,128]{1,0:T(8,128)(2,1)S(1)}, u32[]{:S(2)}, u32[]{:S(2)}) collective-permute-start(bf16[64,128]{1,0:T(8,128)(2,1)S(1)} %fields.1.refs_0_), channel_id=1, source_target_pairs={{0,3},{1,2},{2,1},{3,0},{4,7},{5,6},{6,5},{7,4},{8,11},{9,10},{10,... | collective-permute-start | bytes 49160 | tf_op jit(solution)/shard_map/ppermute | solution.py:355
  19.9 3.7 %collective-permute-start.3 = (bf16[64,128]{1,0:T(8,128)(2,1)S(1)}, bf16[64,128]{1,0:T(8,128)(2,1)S(1)}, u32[]{:S(2)}, u32[]{:S(2)}) collective-permute-start(bf16[64,128]{1,0:T(8,128)(2,1)S(1)} %fields.1.refs_0_), channel_id=1, source_target_pairs={{0,1},{1,0},{2,3},{3,2},{4,5},{5,4},{6,7},{7,6},{8,9},{9,8},{10,11... | collective-permute-start | bytes 49160 | tf_op jit(solution)/shard_map/ppermute | solution.py:355
  23.6 6.0 %collective-permute-start.7 = (bf16[64,128]{1,0:T(8,128)(2,1)S(1)}, bf16[64,128]{1,0:T(8,128)(2,1)S(1)}, u32[]{:S(2)}, u32[]{:S(2)}) collective-permute-start(bf16[64,128]{1,0:T(8,128)(2,1)S(1)} %total.1.own), channel_id=1, source_target_pairs={{4,8},{8,4},{12,16},{16,12},{20,24},{24,20},{5,9},{9,5},{13,17},{1... | collective-permute-start | bytes 49160 | tf_op jit(solution)/shard_map/ppermute | solution.py:359
  25.9 3.7 %collective-permute-start.6 = (bf16[64,128]{1,0:T(8,128)(2,1)S(1)}, bf16[64,128]{1,0:T(8,128)(2,1)S(1)}, u32[]{:S(2)}, u32[]{:S(2)}) collective-permute-start(bf16[64,128]{1,0:T(8,128)(2,1)S(1)} %total.1.own), channel_id=1, source_target_pairs={{0,4},{4,0},{8,12},{12,8},{16,20},{20,16},{24,28},{28,24},{1,5},{5... | collective-permute-start | bytes 49160 | tf_op jit(solution)/shard_map/ppermute | solution.py:357

commit v3 on v2

--- a/solution.py
+++ b/solution.py
@@ -17,7 +17,8 @@
 LANES = 128
 PAIR = 2 * KF
 BLOCKS = N // LANES
-EDGE = PAIR
+EDGE = KF
+WIDE = 3
 PACK = EDGE + KF + 16
 BF16 = jnp.bfloat16
 F32 = jnp.float32
@@ -44,13 +45,13 @@
         0,
     )
     to_columns = columns.transpose(1, 0, 2, 3).reshape(BLOCKS, PAIR, 2 * LANES)
-    from_columns = to_columns.transpose(0, 2, 1)
+    from_columns = to_columns.transpose(0, 2, 1).reshape(BLOCKS // WIDE, WIDE * 2 * LANES, PAIR)
     low, high = full[:HALO], full[HALO + N :]
     blank = np.zeros((HALO, PAIR), np.float32)
     rims = np.stack(
         [
-            np.concatenate([blank, low[::-1]], 0),
-            np.concatenate([blank, low], 0),
+            np.concatenate([low[::-1], blank], 0),
+            np.concatenate([low, blank], 0),
             np.concatenate([high[::-1], blank], 0),
             np.concatenate([high, blank], 0),
         ]
@@ -90,19 +91,22 @@
     return k ^ step if count == 4 else (k - step) % count
 
 
-def call(body, name, outs, args, specs=None, grid=None, scratch=(), flops=0, moved=0, vmem_bytes=VMEM_LIMIT):
+def call(
+    body, name, outs, args, specs, out_specs=None, scratch=(), flops=0, moved=0, alias=None
+):
     vmem = pl.BlockSpec(memory_space=pltpu.VMEM)
-    extra = {} if grid is None else {"grid": grid}
+    if out_specs is None:
+        out_specs = tuple(vmem for _ in outs) if isinstance(outs, tuple) else vmem
     return pl.pallas_call(
         body,
         name=name,
         out_shape=outs,
         in_specs=specs,
-        out_specs=jax.tree.map(lambda _: vmem, outs),
+        out_specs=out_specs,
         scratch_shapes=list(scratch),
-        compiler_params=pltpu.CompilerParams(vmem_limit_bytes=vmem_bytes),
+        input_output_aliases=alias or {},
+        compiler_params=pltpu.CompilerParams(vmem_limit_bytes=VMEM_LIMIT),
         cost_estimate=pl.CostEstimate(flops=flops, bytes_accessed=moved, transcendentals=0),
-        **extra,
     )(*args)
 
 
@@ -140,7 +144,10 @@
         copy.wait()
     strips = jnp.concatenate([held[:, :LANES], held[:, N - LANES :]], 1)
     both = dot(table[...], strips)
+    left = in_left_half((KF, LANES))
     first, last = both[:, :LANES], both[:, LANES:]
+    first = jnp.where(left, first[:KF], swap_halves(first[KF:]))
+    last = jnp.where(left, swap_halves(last[:KF]), last[KF:])
     mate[:EDGE, :] = jnp.where(odd, first, last).astype(BF16)
     other[:EDGE, :] = jnp.where(odd, last, first).astype(BF16)
     inner.wait()
@@ -171,7 +178,10 @@
     high = jnp.where(tile == tiles - 1, jnp.zeros_like(high), high)
     odd = lax.rem(tile, 2) == 1
     low, high = jnp.where(odd, low, high), jnp.where(odd, high, low)
-    blocks = blocks + dot(packs[1][:EDGE, :], low) + dot(packs[0][:EDGE, :], high)
+    for pack, table in ((packs[1], low), (packs[0], high)):
+        edge = pack[:EDGE, :].astype(F32)
+        edge = jnp.concatenate([edge, swap_halves(edge)], 0).astype(BF16)
+        blocks = blocks + dot(edge, table)
     top, bottom = blocks[:KF], swap_halves(blocks[KF:])
     spectrum = jnp.where(left, top - bottom, -(top + bottom))
     turned = swap_halves(spectrum)
@@ -190,32 +200,35 @@
         stacked = jnp.concatenate([product, other], 0).astype(BF16)
         a_ref[index * row_count : (index + 1) * row_count, :] = dot(rows, stacked).astype(BF16)
     step = 32 if row_count % 32 == 0 else 16
-    e_ref[0] = dot(a_ref[...], to_columns[0])
+    e_ref[0] = dot(a_ref[...], to_columns[0]).astype(BF16)
     for block in range(BLOCKS):
         now = block % 2
+        group, place = divmod(block, WIDE)
         if block + 1 < BLOCKS:
-            e_ref[1 - now] = dot(a_ref[...], to_columns[block + 1])
+            e_ref[1 - now] = dot(a_ref[...], to_columns[block + 1]).astype(BF16)
         for r in range(0, row_count, step):
             total = None
             for index in range(count):
                 at = index * row_count + r
-                real = e_ref[now, at : at + step, :LANES]
-                imag = e_ref[now, at : at + step, LANES:]
+                real = e_ref[now, at : at + step, :LANES].astype(F32)
+                imag = e_ref[now, at : at + step, LANES:].astype(F32)
                 term = real * real + imag * imag
                 total = term if total is None else total + term
             wanted = target[r : r + step, block * LANES : (block + 1) * LANES].astype(F32)
             bend = jnp.tanh(total - 2.0)
-            slope = (bend + (1.0 - 2.0 * wanted)) * (1.0 - bend * bend)
+            slope = ((bend + (1.0 - 2.0 * wanted)) * (1.0 - bend * bend)).astype(BF16)
             for index in range(count):
                 at = index * row_count + r
-                for half in (slice(0, LANES), slice(LANES, 2 * LANES)):
-                    field = e_ref[now, at : at + step, half]
-                    v_ref[now, at : at + step, half] = (field * slope).astype(BF16)
-        part = dot(v_ref[now], from_columns[block])
-        if block == 0:
-            u_ref[...] = part
-        else:
-            u_ref[...] += part
+                for half in range(2):
+                    field = e_ref[now, at : at + step, half * LANES : (half + 1) * LANES]
+                    column = (2 * place + half) * LANES
+                    v_ref[group % 2, at : at + step, column : column + LANES] = field * slope
+        if place == WIDE - 1:
+            part = dot(v_ref[group % 2], from_columns[group])
+            if group == 0:
+                u_ref[...] = part
+            else:
+                u_ref[...] += part
     wide = jnp.concatenate(
         [u_ref[i * row_count : (i + 1) * row_count, :].astype(BF16) for i in range(count)], 1
     )
@@ -239,27 +252,56 @@
     refs[count][...] = total.astype(BF16)
 
 
-def gradient_body(row_count, own, near, far, near_pack, far_pack, mid, back, margins, out):
-    left = in_left_half((KF, PAIR))
+def row_waves(rows, pair):
+    pair = pair.astype(F32)
+    other = swap_halves(pair)
+    other = jnp.where(in_left_half(pair.shape), -other, other)
+    return dot(rows, jnp.concatenate([pair, other], 0).astype(BF16)).astype(BF16)
+
+
+def own_rows(mid, row_count):
     begin = pl.multiple_of(lax.axis_index("kern") * row_count, row_count)
-    rows = mid[pl.ds(begin, row_count), :]
-    waves = []
-    for ref in (own, near, far):
-        pair = ref[...].astype(F32)
-        other = swap_halves(pair)
-        other = jnp.where(left, -other, other)
-        waves.append(dot(rows, jnp.concatenate([pair, other], 0).astype(BF16)).astype(BF16))
+    return mid[pl.ds(begin, row_count), :]
+
+
+def inner_body(row_count, own, mid, back, out, waves, held, sems):
+    wave = row_waves(own_rows(mid, row_count), own[...])
+    waves[...] = wave
+    half = BLOCKS // 2 * LANES
+    copies = []
+    for index, (first, last) in enumerate(((0, half), (half, N - 2 * LANES))):
+        held[:, first:last] = dot(wave, back[:, LANES + first : LANES + last])
+        copies.append(
+            pltpu.make_async_copy(
+                held.at[:, first:last], out.at[:, LANES + first : LANES + last], sems.at[index]
+            )
+        )
+        copies[-1].start()
+    for copy in copies:
+        copy.wait()
+
+
+def outer_body(
+    row_count, near, far, near_pack, far_pack, mid, back, margins, waves, begun, out, held, sems
+):
+    rows = own_rows(mid, row_count)
+    near_wave, far_wave = row_waves(rows, near[...]), row_waves(rows, far[...])
     odd = lax.rem(lax.axis_index("tile"), 2) == 1
-    below, above = jnp.where(odd, waves[1], waves[2]), jnp.where(odd, waves[2], waves[1])
+    below, above = jnp.where(odd, near_wave, far_wave), jnp.where(odd, far_wave, near_wave)
     near_marks = near_pack[EDGE + KF :, :].astype(F32)
     far_marks = far_pack[EDGE + KF :, :].astype(F32)
     low_mark = jnp.where(odd, near_marks, far_marks)[1:2]
     high_mark = jnp.where(odd, far_marks, near_marks)[0:1]
     low = jnp.where(low_mark == 1.0, margins[1].astype(F32), margins[0].astype(F32)).astype(BF16)
     high = jnp.where(high_mark == 1.0, margins[3].astype(F32), margins[2].astype(F32)).astype(BF16)
-    out[:, :LANES] = dot(waves[0], back[:, :LANES]) + dot(below, low)
-    out[:, LANES : N - LANES] = dot(waves[0], back[:, LANES : N - LANES])
-    out[:, N - LANES :] = dot(waves[0], back[:, N - LANES :]) + dot(above, high)
+    copies = []
+    for side, first, wave, table in ((0, 0, below, low), (1, N - LANES, above, high)):
+        columns = slice(first, first + LANES)
+        held[side] = dot(waves[...], back[:, columns]) + dot(wave, table)
+        copies.append(pltpu.make_async_copy(held.at[side], out.at[:, columns], sems.at[side]))
+        copies[-1].start()
+    for copy in copies:
+        copy.wait()
 
 
 def far_off(array):
@@ -341,8 +383,8 @@
         [smem] + [vmem] * (7 + count - 1),
         scratch=[
             pltpu.VMEM((count * row_count, PAIR), BF16),
-            pltpu.VMEM((2, count * row_count, 2 * LANES), F32),
             pltpu.VMEM((2, count * row_count, 2 * LANES), BF16),
+            pltpu.VMEM((2, count * row_count, 2 * WIDE * LANES), BF16),
             pltpu.VMEM((count * row_count, PAIR), F32),
         ],
         flops=8 * count * row_count * N * PAIR,
@@ -357,14 +399,34 @@
     near = lax.ppermute(own, "tile", [(t, chip_mate(t)) for t in range(tiles)])
     inner = [t for t in range(tiles) if 0 < t < tiles - 1]
     far = lax.ppermute(own, "tile", [(t, other_side(t)) for t in inner])
+    begun, waves = call(
+        functools.partial(inner_body, row_count),
+        "inner",
+        (jax.ShapeDtypeStruct((row_count, N), F32), pltpu.VMEM((row_count, PAIR), BF16)),
+        (own, mid, back),
+        [vmem] * 3,
+        (hbm, vmem),
+        scratch=[
+            pltpu.VMEM((row_count, N - 2 * LANES), F32),
+            pltpu.SemaphoreType.DMA((2,)),
+        ],
+        flops=2 * row_count * PAIR * N,
+        moved=4 * row_count * N,
+    )
     return call(
-        functools.partial(gradient_body, row_count),
-        "gradient",
+        functools.partial(outer_body, row_count),
+        "outer",
         jax.ShapeDtypeStruct((row_count, N), F32),
-        (own, near, far, packs[1], packs[0], mid, back, margins),
-        [vmem] * 8,
-        flops=2 * row_count * PAIR * (N + 5 * PAIR),
-        moved=4 * row_count * N,
+        (near, far, packs[1], packs[0], mid, back, margins, waves, begun),
+        [vmem] * 8 + [hbm],
+        hbm,
+        scratch=[
+            pltpu.VMEM((2, row_count, LANES), F32),
+            pltpu.SemaphoreType.DMA((2,)),
+        ],
+        flops=2 * row_count * PAIR * 6 * PAIR,
+        moved=4 * row_count * 2 * LANES,
+        alias={8: 0},
     )
 
 

time: 31.4 us -> 30.8 us (0.981)
  waiting for transfers between devices: 8.94 us -> 7.6 us
  Pallas kernels: 9.71 us -> 10.8 us
  starting transfers between devices: 11.8 us -> 11.4 us
    pallas_call x5 -> x6, Pallas kernels: 9.71 us -> 10.8 us  [call(): pl.pallas_call(body, name=name, out_shape=outs, in_specs=specs, out_specs...]
    ppermute x1, waiting for transfers between devices: 2.83 us -> 1.8 us  [per_device(): far = lax.ppermute(own, 'tile', [(t, other_side(t)) for t in inner])]
    ppermute x1, starting transfers between devices: 0.89 us -> 0.41 us  [per_device(): near = lax.ppermute(own, 'tile', [(t, chip_mate(t)) for t in range(tiles)])]
  transfers between devices with their start and end apart: 8 -> 8, of which waited for: 6 -> 6; matrix products, arithmetic and copies ran while one was open for 0% -> 0% of each run, Pallas kernels for 3% -> 8%
where the time goes in v3:
time: 30.8 us; the launch traced here: 30.6 us
  starting transfers between devices  11.4 us (37%)
  Pallas kernels  10.8 us (35%)
  waiting for transfers between devices  7.6 us (25%)
  between operations  0.76 us (2%)
    pallas_call x6, Pallas kernels, call(): pl.pallas_call(body, name=name, out_shape=outs, in_specs=specs, out_specs...  10.8 us
    ppermute x3, starting transfers between devices, per_device(): lax.ppermute(value, ('tile', 'kern'), swapped(move_tile, step))  5.1 us
    ppermute x3, starting transfers between devices, per_device(): parts.append(lax.ppermute(part, 'kern', pairs))  3.55 us
    ppermute x3, waiting for transfers between devices, per_device(): lax.ppermute(value, ('tile', 'kern'), swapped(move_tile, step))  3.2 us
    ppermute x3, waiting for transfers between devices, per_device(): parts.append(lax.ppermute(part, 'kern', pairs))  2.59 us
    ppermute x1, starting transfers between devices, per_device(): far = lax.ppermute(own, 'tile', [(t, other_side(t)) for t in inner])  2.35 us
    ppermute x1, waiting for transfers between devices, per_device(): far = lax.ppermute(own, 'tile', [(t, other_side(t)) for t in inner])  1.8 us
  transfers between devices with their start and end apart: 8, of which 6 were waited for; matrix products, arithmetic and copies ran while one was open for 0% of the time, Pallas kernels for 8%

profile of v3, /device:TPU:4, one launch (start us, length us, event | category | flops | bytes accessed | tf_op | source)
XLA Modules:
  0.0 30.6 jit_solution(2834117974036855085)
XLA Ops:
  0.7 2.0 %edges.1 = (bf16[144,128]{1,0:T(8,128)(2,1)S(1)}, bf16[144,128]{1,0:T(8,128)(2,1)S(1)}, bf16[64,128]{1,0:T(8,128)(2,1)S(1)}, bf16[1152,1152]{1,0:T(8,128)(2,1)S(...) custom-call(bf16[1152,1152]{1,0:T(8,128)(2,1)} %mask.1, bf16[1152,128]{1,0:T(8,128)(2,1)} %constant.14.clone.mid, ...), custom_call_target="tpu_custom_call" | custom-call | flops 75497472 | bytes 589824 | tf_op jit(solution)/shard_map/edges/pallas_call | solution.py:100
  2.7 2.7 %collective-permute-start.2 = (bf16[64,128]{1,0:T(8,128)(2,1)S(1)}, bf16[64,128]{1,0:T(8,128)(2,1)S(1)}, u32[]{:S(2)}, u32[]{:S(2)}) collective-permute-start(bf16[64,128]{1,0:T(8,128)(2,1)S(1)} %get-tuple-element.16.refs_7_), channel_id=1, source_target_pairs={{0,2},{1,3},{2,0},{3,1},{4,6},{5,7},{6,4},{7,5},{8,10},{9,11},{10,... | collective-permute-start | bytes 49160 | tf_op jit(solution)/shard_map/ppermute | solution.py:366
  5.3 1.6 %collective-permute-start = (bf16[144,128]{1,0:T(8,128)(2,1)S(1)}, bf16[144,128]{1,0:T(8,128)(2,1)S(1)}, u32[]{:S(2)}, u32[]{:S(2)}) collective-permute-start(bf16[144,128]{1,0:T(8,128)(2,1)S(1)} %get-tuple-element.17), channel_id=1, source_target_pairs={{0,29},{1,28},{2,31},{3,30},{4,9},{5,8},{6,11},{7,10},{8,5},{9,4},... | collective-permute-start | bytes 110600 | tf_op jit(solution)/shard_map/ppermute | solution.py:366
  6.9 0.8 %collective-permute-start.1 = (bf16[144,128]{1,0:T(8,128)(2,1)S(1)}, bf16[144,128]{1,0:T(8,128)(2,1)S(1)}, u32[]{:S(2)}, u32[]{:S(2)}) collective-permute-start(bf16[144,128]{1,0:T(8,128)(2,1)S(1)} %get-tuple-element.18), channel_id=1, source_target_pairs={{0,7},{1,6},{2,5},{3,4},{4,3},{5,2},{6,1},{7,0},{8,15},{9,14},{10,... | collective-permute-start | bytes 110600 | tf_op jit(solution)/shard_map/ppermute | solution.py:366
  7.8 0.0 copy-start.2
  7.8 0.0 copy-start.6
  7.8 1.1 %middle.1.refs_1_ = f32[128,128]{1,0:T(8,128)S(1)} custom-call(bf16[1152,1152]{1,0:T(8,128)(2,1)S(1)} %get-tuple-element.13.mask, bf16[1152,128]{1,0:T(8,128)(2,1)S(1)} %get-tuple-element.14.mid.refs_3_, bf16[128,1152]{1,0:T(8,128)(2,1)S(1)} %get-tuple-element.15.mid_t), custom_call_target="tpu_custom_call" | custom-call | flops 679477248 | bytes 2654208 | tf_op jit(solution)/shard_map/middle/pallas_call | solution.py:100
  8.9 0.0 copy-start
  8.9 0.0 copy-start.1
  8.9 0.0 collective-permute-done.2.refs_10_
  8.9 1.6 %collective-permute-done.refs_8_.far_pack = bf16[144,128]{1,0:T(8,128)(2,1)S(1)} collective-permute-done((bf16[144,128]{1,0:T(8,128)(2,1)S(1)}, bf16[144,128]{1,0:T(8,128)(2,1)S(1)}, u32[]{:S(2)}, u32[]{:S(2)}) %collective-permute-start) | collective-permute-done | bytes 36896 | tf_op jit(solution)/shard_map/ppermute | solution.py:366
  10.5 1.6 %collective-permute-done.1.refs_9_.near_pack = bf16[144,128]{1,0:T(8,128)(2,1)S(1)} collective-permute-done((bf16[144,128]{1,0:T(8,128)(2,1)S(1)}, bf16[144,128]{1,0:T(8,128)(2,1)S(1)}, u32[]{:S(2)}, u32[]{:S(2)}) %collective-permute-start.1) | collective-permute-done | bytes 36896 | tf_op jit(solution)/shard_map/ppermute | solution.py:366
  12.1 0.0 copy-done.2
  12.1 0.0 copy-done.3
  12.1 0.0 copy-done.4
  12.1 0.0 copy-done.5
  12.1 0.0 copy-done.6
  12.1 5.2 %fields.1.refs_0_ = bf16[64,128]{1,0:T(8,128)(2,1)S(1)} custom-call(s32[1,2]{1,0:T(1,128)S(1)} %copy-done.2, f32[128,128]{1,0:T(8,128)S(1)} %middle.1.refs_1_, s32[288,1152]{1,0:T(8,128)S(1)} %copy-done.3, bf16[1152,128]{1,0:T(8,128)(2,1)S(1)} %get-tuple-element.14.mid.refs_3_, bf16[9,128,256]{2,1,0:T(8,128)(2,1)S(1)} %copy-done.5, ...), custom_call_target="tpu_custom_call" | custom-call | flops 1358954496 | bytes 1327104 | tf_op jit(solution)/shard_map/fields/pallas_call | solution.py:100
  17.4 0.1 collective-permute-start.5
  17.5 2.3 %collective-permute-start.4 = (bf16[64,128]{1,0:T(8,128)(2,1)S(1)}, bf16[64,128]{1,0:T(8,128)(2,1)S(1)}, u32[]{:S(2)}, u32[]{:S(2)}) collective-permute-start(bf16[64,128]{1,0:T(8,128)(2,1)S(1)} %fields.1.refs_0_), channel_id=1, source_target_pairs={{0,3},{1,2},{2,1},{3,0},{4,7},{5,6},{6,5},{7,4},{8,11},{9,10},{10,... | collective-permute-start | bytes 49160 | tf_op jit(solution)/shard_map/ppermute | solution.py:397
  19.8 1.1 %collective-permute-start.3 = (bf16[64,128]{1,0:T(8,128)(2,1)S(1)}, bf16[64,128]{1,0:T(8,128)(2,1)S(1)}, u32[]{:S(2)}, u32[]{:S(2)}) collective-permute-start(bf16[64,128]{1,0:T(8,128)(2,1)S(1)} %fields.1.refs_0_), channel_id=1, source_target_pairs={{0,1},{1,0},{2,3},{3,2},{4,5},{5,4},{6,7},{7,6},{8,9},{9,8},{10,11... | collective-permute-start | bytes 49160 | tf_op jit(solution)/shard_map/ppermute | solution.py:397
  20.9 1.3 %collective-permute-done.5.refs_3_ = bf16[64,128]{1,0:T(8,128)(2,1)S(1)} collective-permute-done((bf16[64,128]{1,0:T(8,128)(2,1)S(1)}, bf16[64,128]{1,0:T(8,128)(2,1)S(1)}, u32[]{:S(2)}, u32[]{:S(2)}) %collective-permute-start.5) | collective-permute-done | bytes 16416 | tf_op jit(solution)/shard_map/ppermute | solution.py:397
  22.2 1.0 %collective-permute-done.4.refs_2_ = bf16[64,128]{1,0:T(8,128)(2,1)S(1)} collective-permute-done((bf16[64,128]{1,0:T(8,128)(2,1)S(1)}, bf16[64,128]{1,0:T(8,128)(2,1)S(1)}, u32[]{:S(2)}, u32[]{:S(2)}) %collective-permute-start.4) | collective-permute-done | bytes 16416 | tf_op jit(solution)/shard_map/ppermute | solution.py:397
  23.3 0.3 collective-permute-done.3.refs_1_
  23.5 2.3 %collective-permute-start.7 = (bf16[64,128]{1,0:T(8,128)(2,1)S(1)}, bf16[64,128]{1,0:T(8,128)(2,1)S(1)}, u32[]{:S(2)}, u32[]{:S(2)}) collective-permute-start(bf16[64,128]{1,0:T(8,128)(2,1)S(1)} %total.1.own), channel_id=1, source_target_pairs={{4,8},{8,4},{12,16},{16,12},{20,24},{24,20},{5,9},{9,5},{13,17},{1... | collective-permute-start | bytes 49160 | tf_op jit(solution)/shard_map/ppermute | solution.py:401
  25.9 0.4 %collective-permute-start.6 = (bf16[64,128]{1,0:T(8,128)(2,1)S(1)}, bf16[64,128]{1,0:T(8,128)(2,1)S(1)}, u32[]{:S(2)}, u32[]{:S(2)}) collective-permute-start(bf16[64,128]{1,0:T(8,128)(2,1)S(1)} %total.1.own), channel_id=1, source_target_pairs={{0,4},{4,0},{8,12},{12,8},{16,20},{20,16},{24,28},{28,24},{1,5},{5... | collective-permute-start | bytes 49160 | tf_op jit(solution)/shard_map/ppermute | solution.py:399
  26.3 0.0 copy-done
  26.3 1.4 %inner.1 = (f32[288,1152]{1,0:T(8,128)}, bf16[288,128]{1,0:T(8,128)(2,1)S(1)}) custom-call(bf16[64,128]{1,0:T(8,128)(2,1)S(1)} %total.1.own, bf16[1152,128]{1,0:T(8,128)(2,1)S(1)} %get-tuple-element.14.mid.refs_3_, bf16[128,1152]{1,0:T(8,128)(2,1)S(1)} %copy-done), custom_call_target="tpu_custom_call" | custom-call | flops 84934656 | bytes 1327104 | tf_op jit(solution)/shard_map/inner/pallas_call | solution.py:100
  27.7 1.8 %collective-permute-done.7.far = bf16[64,128]{1,0:T(8,128)(2,1)S(1)} collective-permute-done((bf16[64,128]{1,0:T(8,128)(2,1)S(1)}, bf16[64,128]{1,0:T(8,128)(2,1)S(1)}, u32[]{:S(2)}, u32[]{:S(2)}) %collective-permute-start.7) | collective-permute-done | bytes 16416 | tf_op jit(solution)/shard_map/ppermute | solution.py:401
  29.5 0.0 collective-permute-done.6.near
  29.5 0.0 copy-done.1
  29.5 1.1 %outer.1 = f32[288,1152]{1,0:T(8,128)} custom-call(bf16[64,128]{1,0:T(8,128)(2,1)S(1)} %collective-permute-done.6.near, bf16[64,128]{1,0:T(8,128)(2,1)S(1)} %collective-permute-done.7.far, bf16[144,128]{1,0:T(8,128)(2,1)S(1)} %collective-permute-done.1.refs_9_.near_pack, ...), custom_call_target="tpu_custom_call", output_to_operand_aliasing={{}: (8, {})} | custom-call | flops 56623104 | bytes 294912 | tf_op jit(solution)/shard_map/outer/pallas_call | solution.py:100
  (4 shorter events, 0.0 us)
Async XLA Ops:
  2.7 6.2 %collective-permute-start.2 = (bf16[64,128]{1,0:T(8,128)(2,1)S(1)}, bf16[64,128]{1,0:T(8,128)(2,1)S(1)}, u32[]{:S(2)}, u32[]{:S(2)}) collective-permute-start(bf16[64,128]{1,0:T(8,128)(2,1)S(1)} %get-tuple-element.16.refs_7_), channel_id=1, source_target_pairs={{0,2},{1,3},{2,0},{3,1},{4,6},{5,7},{6,4},{7,5},{8,10},{9,11},{10,... | collective-permute-start | bytes 49160 | tf_op jit(solution)/shard_map/ppermute | solution.py:366
  5.3 5.2 %collective-permute-start = (bf16[144,128]{1,0:T(8,128)(2,1)S(1)}, bf16[144,128]{1,0:T(8,128)(2,1)S(1)}, u32[]{:S(2)}, u32[]{:S(2)}) collective-permute-start(bf16[144,128]{1,0:T(8,128)(2,1)S(1)} %get-tuple-element.17), channel_id=1, source_target_pairs={{0,29},{1,28},{2,31},{3,30},{4,9},{5,8},{6,11},{7,10},{8,5},{9,4},... | collective-permute-start | bytes 110600 | tf_op jit(solution)/shard_map/ppermute | solution.py:366
  6.9 5.2 %collective-permute-start.1 = (bf16[144,128]{1,0:T(8,128)(2,1)S(1)}, bf16[144,128]{1,0:T(8,128)(2,1)S(1)}, u32[]{:S(2)}, u32[]{:S(2)}) collective-permute-start(bf16[144,128]{1,0:T(8,128)(2,1)S(1)} %get-tuple-element.18), channel_id=1, source_target_pairs={{0,7},{1,6},{2,5},{3,4},{4,3},{5,2},{6,1},{7,0},{8,15},{9,14},{10,... | collective-permute-start | bytes 110600 | tf_op jit(solution)/shard_map/ppermute | solution.py:366
  7.8 4.3 %copy-start.2 = (s32[1,2]{1,0:T(1,128)S(1)}, s32[1,2]{1,0:T(1,128)}, u32[]{:S(2)}) copy-start(s32[1,2]{1,0:T(1,128)} %refs_0_.1) | copy-start | bytes 28
  7.8 4.3 %copy-start.3 = (s32[288,1152]{1,0:T(8,128)S(1)}, s32[288,1152]{1,0:T(8,128)}, u32[]{:S(2)}) copy-start(s32[288,1152]{1,0:T(8,128)} %refs_2_.1) | copy-start | bytes 3981316
  7.8 4.3 %copy-start.4 = (bf16[3,768,128]{2,1,0:T(8,128)(2,1)S(1)}, bf16[3,768,128]{2,1,0:T(8,128)(2,1)}, u32[]{:S(2)}) copy-start(bf16[3,768,128]{2,1,0:T(8,128)(2,1)} %constant.17.clone.refs_5_) | copy-start | bytes 1769476
  7.8 4.3 %copy-start.5 = (bf16[9,128,256]{2,1,0:T(8,128)(2,1)S(1)}, bf16[9,128,256]{2,1,0:T(8,128)(2,1)}, u32[]{:S(2)}) copy-start(bf16[9,128,256]{2,1,0:T(8,128)(2,1)} %constant.16.clone.refs_4_) | copy-start | bytes 1769476
  7.8 4.4 %copy-start.6 = (bf16[4,128,128]{2,1,0:T(8,128)(2,1)S(1)}, bf16[4,128,128]{2,1,0:T(8,128)(2,1)}, u32[]{:S(2)}) copy-start(bf16[4,128,128]{2,1,0:T(8,128)(2,1)} %constant.18.clone.refs_6_) | copy-start | bytes 393220
  8.9 17.4 %copy-start = (bf16[128,1152]{1,0:T(8,128)(2,1)S(1)}, bf16[128,1152]{1,0:T(8,128)(2,1)}, u32[]{:S(2)}) copy-start(bf16[128,1152]{1,0:T(8,128)(2,1)} %constant.19.clone.back) | copy-start | bytes 884740
  8.9 20.6 %copy-start.1 = (bf16[4,128,128]{2,1,0:T(8,128)(2,1)S(1)}, bf16[4,128,128]{2,1,0:T(8,128)(2,1)}, u32[]{:S(2)}) copy-start(bf16[4,128,128]{2,1,0:T(8,128)(2,1)} %constant.20.clone.margins) | copy-start | bytes 393220
  17.4 4.8 %collective-permute-start.5 = (bf16[64,128]{1,0:T(8,128)(2,1)S(1)}, bf16[64,128]{1,0:T(8,128)(2,1)S(1)}, u32[]{:S(2)}, u32[]{:S(2)}) collective-permute-start(bf16[64,128]{1,0:T(8,128)(2,1)S(1)} %fields.1.refs_0_), channel_id=1, source_target_pairs={{0,2},{1,3},{2,0},{3,1},{4,6},{5,7},{6,4},{7,5},{8,10},{9,11},{10,... | collective-permute-start | bytes 49160 | tf_op jit(solution)/shard_map/ppermute | solution.py:397
  17.5 5.8 %collective-permute-start.4 = (bf16[64,128]{1,0:T(8,128)(2,1)S(1)}, bf16[64,128]{1,0:T(8,128)(2,1)S(1)}, u32[]{:S(2)}, u32[]{:S(2)}) collective-permute-start(bf16[64,128]{1,0:T(8,128)(2,1)S(1)} %fields.1.refs_0_), channel_id=1, source_target_pairs={{0,3},{1,2},{2,1},{3,0},{4,7},{5,6},{6,5},{7,4},{8,11},{9,10},{10,... | collective-permute-start | bytes 49160 | tf_op jit(solution)/shard_map/ppermute | solution.py:397
  19.8 3.7 %collective-permute-start.3 = (bf16[64,128]{1,0:T(8,128)(2,1)S(1)}, bf16[64,128]{1,0:T(8,128)(2,1)S(1)}, u32[]{:S(2)}, u32[]{:S(2)}) collective-permute-start(bf16[64,128]{1,0:T(8,128)(2,1)S(1)} %fields.1.refs_0_), channel_id=1, source_target_pairs={{0,1},{1,0},{2,3},{3,2},{4,5},{5,4},{6,7},{7,6},{8,9},{9,8},{10,11... | collective-permute-start | bytes 49160 | tf_op jit(solution)/shard_map/ppermute | solution.py:397
  23.5 6.0 %collective-permute-start.7 = (bf16[64,128]{1,0:T(8,128)(2,1)S(1)}, bf16[64,128]{1,0:T(8,128)(2,1)S(1)}, u32[]{:S(2)}, u32[]{:S(2)}) collective-permute-start(bf16[64,128]{1,0:T(8,128)(2,1)S(1)} %total.1.own), channel_id=1, source_target_pairs={{4,8},{8,4},{12,16},{16,12},{20,24},{24,20},{5,9},{9,5},{13,17},{1... | collective-permute-start | bytes 49160 | tf_op jit(solution)/shard_map/ppermute | solution.py:401
  25.9 3.6 %collective-permute-start.6 = (bf16[64,128]{1,0:T(8,128)(2,1)S(1)}, bf16[64,128]{1,0:T(8,128)(2,1)S(1)}, u32[]{:S(2)}, u32[]{:S(2)}) collective-permute-start(bf16[64,128]{1,0:T(8,128)(2,1)S(1)} %total.1.own), channel_id=1, source_target_pairs={{0,4},{4,0},{8,12},{12,8},{16,20},{20,16},{24,28},{28,24},{1,5},{5... | collective-permute-start | bytes 49160 | tf_op jit(solution)/shard_map/ppermute | solution.py:399

commit v4 on v3

--- a/solution.py
+++ b/solution.py
@@ -18,7 +18,6 @@
 PAIR = 2 * KF
 BLOCKS = N // LANES
 EDGE = KF
-WIDE = 3
 PACK = EDGE + KF + 16
 BF16 = jnp.bfloat16
 F32 = jnp.float32
@@ -45,7 +44,7 @@
         0,
     )
     to_columns = columns.transpose(1, 0, 2, 3).reshape(BLOCKS, PAIR, 2 * LANES)
-    from_columns = to_columns.transpose(0, 2, 1).reshape(BLOCKS // WIDE, WIDE * 2 * LANES, PAIR)
+    from_columns = to_columns.transpose(0, 2, 1)
     low, high = full[:HALO], full[HALO + N :]
     blank = np.zeros((HALO, PAIR), np.float32)
     rims = np.stack(
@@ -200,35 +199,35 @@
         stacked = jnp.concatenate([product, other], 0).astype(BF16)
         a_ref[index * row_count : (index + 1) * row_count, :] = dot(rows, stacked).astype(BF16)
     step = 32 if row_count % 32 == 0 else 16
+    steps = list(range(0, row_count, step))
+    shares = [steps[i * len(steps) // count : (i + 1) * len(steps) // count] for i in range(count)]
     e_ref[0] = dot(a_ref[...], to_columns[0]).astype(BF16)
-    for block in range(BLOCKS):
+    for block in range(BLOCKS + 1):
         now = block % 2
-        group, place = divmod(block, WIDE)
-        if block + 1 < BLOCKS:
-            e_ref[1 - now] = dot(a_ref[...], to_columns[block + 1]).astype(BF16)
-        for r in range(0, row_count, step):
-            total = None
-            for index in range(count):
-                at = index * row_count + r
-                real = e_ref[now, at : at + step, :LANES].astype(F32)
-                imag = e_ref[now, at : at + step, LANES:].astype(F32)
-                term = real * real + imag * imag
-                total = term if total is None else total + term
-            wanted = target[r : r + step, block * LANES : (block + 1) * LANES].astype(F32)
-            bend = jnp.tanh(total - 2.0)
-            slope = ((bend + (1.0 - 2.0 * wanted)) * (1.0 - bend * bend)).astype(BF16)
-            for index in range(count):
-                at = index * row_count + r
-                for half in range(2):
-                    field = e_ref[now, at : at + step, half * LANES : (half + 1) * LANES]
-                    column = (2 * place + half) * LANES
-                    v_ref[group % 2, at : at + step, column : column + LANES] = field * slope
-        if place == WIDE - 1:
-            part = dot(v_ref[group % 2], from_columns[group])
-            if group == 0:
-                u_ref[...] = part
-            else:
-                u_ref[...] += part
+        for share in range(count):
+            mine = slice(share * row_count, (share + 1) * row_count)
+            if block + 1 < BLOCKS:
+                e_ref[1 - now, mine, :] = dot(a_ref[mine, :], to_columns[block + 1]).astype(BF16)
+            if block > 0:
+                part = dot(v_ref[1 - now, mine, :], from_columns[block - 1])
+                u_ref[mine, :] = part if block == 1 else u_ref[mine, :] + part
+            if block == BLOCKS:
+                continue
+            for r in shares[share]:
+                total = None
+                for index in range(count):
+                    at = index * row_count + r
+                    real = e_ref[now, at : at + step, :LANES]
+                    imag = e_ref[now, at : at + step, LANES:]
+                    term = (real * real + imag * imag).astype(F32)
+                    total = term if total is None else total + term
+                wanted = target[r : r + step, block * LANES : (block + 1) * LANES].astype(F32)
+                bend = jnp.tanh(total - 2.0)
+                slope = ((bend + (1.0 - 2.0 * wanted)) * (1.0 - bend * bend)).astype(BF16)
+                for index in range(count):
+                    at = index * row_count + r
+                    for half in (slice(0, LANES), slice(LANES, 2 * LANES)):
+                        v_ref[now, at : at + step, half] = e_ref[now, at : at + step, half] * slope
     wide = jnp.concatenate(
         [u_ref[i * row_count : (i + 1) * row_count, :].astype(BF16) for i in range(count)], 1
     )
@@ -384,18 +383,27 @@
         scratch=[
             pltpu.VMEM((count * row_count, PAIR), BF16),
             pltpu.VMEM((2, count * row_count, 2 * LANES), BF16),
-            pltpu.VMEM((2, count * row_count, 2 * WIDE * LANES), BF16),
+            pltpu.VMEM((2, count * row_count, 2 * LANES), BF16),
             pltpu.VMEM((count * row_count, PAIR), F32),
         ],
         flops=8 * count * row_count * N * PAIR,
         moved=4 * row_count * N,
     )
 
-    parts = [part]
-    for step in kern_steps(count):
+    def summed(parts):
+        return call(
+            functools.partial(sum_body, len(parts)), "total", small, parts, [vmem] * len(parts)
+        )
+
+    def moved(value, step):
         pairs = [(k, destination(k, step, count)) for k in range(count)]
-        parts.append(lax.ppermute(part, "kern", pairs))
-    own = call(functools.partial(sum_body, count), "total", small, tuple(parts), [vmem] * count)
+        return lax.ppermute(value, "kern", pairs)
+
+    if count == 4:
+        own = summed((part, moved(part, 1)))
+        own = summed((own, moved(own, 2)))
+    else:
+        own = summed((part, *(moved(part, step) for step in kern_steps(count))))
     near = lax.ppermute(own, "tile", [(t, chip_mate(t)) for t in range(tiles)])
     inner = [t for t in range(tiles) if 0 < t < tiles - 1]
     far = lax.ppermute(own, "tile", [(t, other_side(t)) for t in inner])

time: 30.8 us -> 33.2 us (1.078)
  waiting for transfers between devices: 7.6 us -> 13.4 us
  starting transfers between devices: 11.4 us -> 7.98 us
    ppermute x3 -> x2, waiting for transfers between devices: 2.59 us -> 8.32 us  [moved(): return lax.ppermute(value, 'kern', pairs)]
    ppermute x3 -> x2, starting transfers between devices: 3.55 us -> 0.24 us  [moved(): return lax.ppermute(value, 'kern', pairs)]
    ppermute x1, starting transfers between devices: 2.35 us -> 1.91 us  [per_device(): far = lax.ppermute(own, 'tile', [(t, other_side(t)) for t in inner])]
    pallas_call x6 -> x7, Pallas kernels: 10.8 us -> 10.8 us  [call(): pl.pallas_call(body, name=name, out_shape=outs, in_specs=specs, out_specs...]
  transfers between devices with their start and end apart: 8 -> 7, of which waited for: 6 -> 5; matrix products, arithmetic and copies ran while one was open for 0% -> 0% of each run, Pallas kernels for 8% -> 7%
where the time goes in v4:
time: 33.2 us; the launch traced here: 33 us
  waiting for transfers between devices  13.4 us (40%)
  Pallas kernels  10.8 us (33%)
  starting transfers between devices  7.98 us (24%)
  between operations  0.76 us (2%)
    pallas_call x7, Pallas kernels, call(): pl.pallas_call(body, name=name, out_shape=outs, in_specs=specs, out_specs...  10.8 us
    ppermute x2, waiting for transfers between devices, moved(): return lax.ppermute(value, 'kern', pairs)  8.32 us
    ppermute x3, starting transfers between devices, per_device(): lax.ppermute(value, ('tile', 'kern'), swapped(move_tile, step))  5.1 us
    ppermute x3, waiting for transfers between devices, per_device(): lax.ppermute(value, ('tile', 'kern'), swapped(move_tile, step))  3.2 us
    ppermute x1, starting transfers between devices, per_device(): far = lax.ppermute(own, 'tile', [(t, other_side(t)) for t in inner])  1.91 us
    ppermute x1, waiting for transfers between devices, per_device(): far = lax.ppermute(own, 'tile', [(t, other_side(t)) for t in inner])  1.9 us
    ppermute x1, starting transfers between devices, per_device(): near = lax.ppermute(own, 'tile', [(t, chip_mate(t)) for t in range(tiles)])  0.73 us
  transfers between devices with their start and end apart: 7, of which 5 were waited for; matrix products, arithmetic and copies ran while one was open for 0% of the time, Pallas kernels for 7%

profile of v4, /device:TPU:4, one launch (start us, length us, event | category | flops | bytes accessed | tf_op | source)
XLA Modules:
  0.0 33.0 jit_solution(157824111775253628)
XLA Ops:
  0.7 2.0 %edges.1 = (bf16[144,128]{1,0:T(8,128)(2,1)S(1)}, bf16[144,128]{1,0:T(8,128)(2,1)S(1)}, bf16[64,128]{1,0:T(8,128)(2,1)S(1)}, bf16[1152,1152]{1,0:T(8,128)(2,1)S(...) custom-call(bf16[1152,1152]{1,0:T(8,128)(2,1)} %mask.1, bf16[1152,128]{1,0:T(8,128)(2,1)} %constant.14.clone.mid, ...), custom_call_target="tpu_custom_call" | custom-call | flops 75497472 | bytes 589824 | tf_op jit(solution)/shard_map/edges/pallas_call | solution.py:99
  2.7 2.7 %collective-permute-start.2 = (bf16[64,128]{1,0:T(8,128)(2,1)S(1)}, bf16[64,128]{1,0:T(8,128)(2,1)S(1)}, u32[]{:S(2)}, u32[]{:S(2)}) collective-permute-start(bf16[64,128]{1,0:T(8,128)(2,1)S(1)} %get-tuple-element.16.refs_7_), channel_id=1, source_target_pairs={{0,2},{1,3},{2,0},{3,1},{4,6},{5,7},{6,4},{7,5},{8,10},{9,11},{10,... | collective-permute-start | bytes 49160 | tf_op jit(solution)/shard_map/ppermute | solution.py:365
  5.3 1.6 %collective-permute-start = (bf16[144,128]{1,0:T(8,128)(2,1)S(1)}, bf16[144,128]{1,0:T(8,128)(2,1)S(1)}, u32[]{:S(2)}, u32[]{:S(2)}) collective-permute-start(bf16[144,128]{1,0:T(8,128)(2,1)S(1)} %get-tuple-element.17), channel_id=1, source_target_pairs={{0,29},{1,28},{2,31},{3,30},{4,9},{5,8},{6,11},{7,10},{8,5},{9,4},... | collective-permute-start | bytes 110600 | tf_op jit(solution)/shard_map/ppermute | solution.py:365
  6.9 0.8 %collective-permute-start.1 = (bf16[144,128]{1,0:T(8,128)(2,1)S(1)}, bf16[144,128]{1,0:T(8,128)(2,1)S(1)}, u32[]{:S(2)}, u32[]{:S(2)}) collective-permute-start(bf16[144,128]{1,0:T(8,128)(2,1)S(1)} %get-tuple-element.18), channel_id=1, source_target_pairs={{0,7},{1,6},{2,5},{3,4},{4,3},{5,2},{6,1},{7,0},{8,15},{9,14},{10,... | collective-permute-start | bytes 110600 | tf_op jit(solution)/shard_map/ppermute | solution.py:365
  7.8 0.0 copy-start.2
  7.8 0.0 copy-start.3
  7.8 0.0 copy-start.4
  7.8 0.0 copy-start.6
  7.8 1.1 %middle.1.refs_1_ = f32[128,128]{1,0:T(8,128)S(1)} custom-call(bf16[1152,1152]{1,0:T(8,128)(2,1)S(1)} %get-tuple-element.13.mask, bf16[1152,128]{1,0:T(8,128)(2,1)S(1)} %get-tuple-element.14.mid.refs_3_, bf16[128,1152]{1,0:T(8,128)(2,1)S(1)} %get-tuple-element.15.mid_t), custom_call_target="tpu_custom_call" | custom-call | flops 679477248 | bytes 2654208 | tf_op jit(solution)/shard_map/middle/pallas_call | solution.py:99
  8.9 0.0 copy-start
  8.9 0.0 copy-start.1
  8.9 0.0 collective-permute-done.2.refs_10_
  8.9 1.6 %collective-permute-done.refs_8_.far_pack = bf16[144,128]{1,0:T(8,128)(2,1)S(1)} collective-permute-done((bf16[144,128]{1,0:T(8,128)(2,1)S(1)}, bf16[144,128]{1,0:T(8,128)(2,1)S(1)}, u32[]{:S(2)}, u32[]{:S(2)}) %collective-permute-start) | collective-permute-done | bytes 36896 | tf_op jit(solution)/shard_map/ppermute | solution.py:365
  10.5 1.6 %collective-permute-done.1.refs_9_.near_pack = bf16[144,128]{1,0:T(8,128)(2,1)S(1)} collective-permute-done((bf16[144,128]{1,0:T(8,128)(2,1)S(1)}, bf16[144,128]{1,0:T(8,128)(2,1)S(1)}, u32[]{:S(2)}, u32[]{:S(2)}) %collective-permute-start.1) | collective-permute-done | bytes 36896 | tf_op jit(solution)/shard_map/ppermute | solution.py:365
  12.1 0.0 copy-done.2
  12.1 0.0 copy-done.3
  12.1 0.0 copy-done.4
  12.1 0.0 copy-done.5
  12.1 0.0 copy-done.6
  12.1 5.2 %fields.1.refs_0_ = bf16[64,128]{1,0:T(8,128)(2,1)S(1)} custom-call(s32[1,2]{1,0:T(1,128)S(1)} %copy-done.2, f32[128,128]{1,0:T(8,128)S(1)} %middle.1.refs_1_, s32[288,1152]{1,0:T(8,128)S(1)} %copy-done.3, bf16[1152,128]{1,0:T(8,128)(2,1)S(1)} %get-tuple-element.14.mid.refs_3_, bf16[9,128,256]{2,1,0:T(8,128)(2,1)S(1)} %copy-done.5, ...), custom_call_target="tpu_custom_call" | custom-call | flops 1358954496 | bytes 1327104 | tf_op jit(solution)/shard_map/fields/pallas_call | solution.py:99
  17.3 0.1 collective-permute-start.3
  17.4 3.9 %collective-permute-done.3.refs_1_ = bf16[64,128]{1,0:T(8,128)(2,1)S(1)} collective-permute-done((bf16[64,128]{1,0:T(8,128)(2,1)S(1)}, bf16[64,128]{1,0:T(8,128)(2,1)S(1)}, u32[]{:S(2)}, u32[]{:S(2)}) %collective-permute-start.3) | collective-permute-done | bytes 16416 | tf_op jit(solution)/shard_map/ppermute | solution.py:400
  21.3 0.2 collective-permute-start.4
  21.5 4.5 %collective-permute-done.4.refs_1_ = bf16[64,128]{1,0:T(8,128)(2,1)S(1)} collective-permute-done((bf16[64,128]{1,0:T(8,128)(2,1)S(1)}, bf16[64,128]{1,0:T(8,128)(2,1)S(1)}, u32[]{:S(2)}, u32[]{:S(2)}) %collective-permute-start.4) | collective-permute-done | bytes 16416 | tf_op jit(solution)/shard_map/ppermute | solution.py:400
  25.9 1.9 %collective-permute-start.6 = (bf16[64,128]{1,0:T(8,128)(2,1)S(1)}, bf16[64,128]{1,0:T(8,128)(2,1)S(1)}, u32[]{:S(2)}, u32[]{:S(2)}) collective-permute-start(bf16[64,128]{1,0:T(8,128)(2,1)S(1)} %total.3.own), channel_id=1, source_target_pairs={{4,8},{8,4},{12,16},{16,12},{20,24},{24,20},{5,9},{9,5},{13,17},{1... | collective-permute-start | bytes 49160 | tf_op jit(solution)/shard_map/ppermute | solution.py:409
  27.9 0.7 %collective-permute-start.5 = (bf16[64,128]{1,0:T(8,128)(2,1)S(1)}, bf16[64,128]{1,0:T(8,128)(2,1)S(1)}, u32[]{:S(2)}, u32[]{:S(2)}) collective-permute-start(bf16[64,128]{1,0:T(8,128)(2,1)S(1)} %total.3.own), channel_id=1, source_target_pairs={{0,4},{4,0},{8,12},{12,8},{16,20},{20,16},{24,28},{28,24},{1,5},{5... | collective-permute-start | bytes 49160 | tf_op jit(solution)/shard_map/ppermute | solution.py:407
  28.6 0.0 copy-done
  28.6 1.4 %inner.1 = (f32[288,1152]{1,0:T(8,128)}, bf16[288,128]{1,0:T(8,128)(2,1)S(1)}) custom-call(bf16[64,128]{1,0:T(8,128)(2,1)S(1)} %total.3.own, bf16[1152,128]{1,0:T(8,128)(2,1)S(1)} %get-tuple-element.14.mid.refs_3_, bf16[128,1152]{1,0:T(8,128)(2,1)S(1)} %copy-done), custom_call_target="tpu_custom_call" | custom-call | flops 84934656 | bytes 1327104 | tf_op jit(solution)/shard_map/inner/pallas_call | solution.py:99
  30.0 1.9 %collective-permute-done.6.far = bf16[64,128]{1,0:T(8,128)(2,1)S(1)} collective-permute-done((bf16[64,128]{1,0:T(8,128)(2,1)S(1)}, bf16[64,128]{1,0:T(8,128)(2,1)S(1)}, u32[]{:S(2)}, u32[]{:S(2)}) %collective-permute-start.6) | collective-permute-done | bytes 16416 | tf_op jit(solution)/shard_map/ppermute | solution.py:409
  31.9 0.0 collective-permute-done.5.near
  31.9 0.0 copy-done.1
  31.9 1.1 %outer.1 = f32[288,1152]{1,0:T(8,128)} custom-call(bf16[64,128]{1,0:T(8,128)(2,1)S(1)} %collective-permute-done.5.near, bf16[64,128]{1,0:T(8,128)(2,1)S(1)} %collective-permute-done.6.far, bf16[144,128]{1,0:T(8,128)(2,1)S(1)} %collective-permute-done.1.refs_9_.near_pack, ...), custom_call_target="tpu_custom_call", output_to_operand_aliasing={{}: (8, {})} | custom-call | flops 56623104 | bytes 294912 | tf_op jit(solution)/shard_map/outer/pallas_call | solution.py:99
  (3 shorter events, 0.0 us)
Async XLA Ops:
  2.7 6.2 %collective-permute-start.2 = (bf16[64,128]{1,0:T(8,128)(2,1)S(1)}, bf16[64,128]{1,0:T(8,128)(2,1)S(1)}, u32[]{:S(2)}, u32[]{:S(2)}) collective-permute-start(bf16[64,128]{1,0:T(8,128)(2,1)S(1)} %get-tuple-element.16.refs_7_), channel_id=1, source_target_pairs={{0,2},{1,3},{2,0},{3,1},{4,6},{5,7},{6,4},{7,5},{8,10},{9,11},{10,... | collective-permute-start | bytes 49160 | tf_op jit(solution)/shard_map/ppermute | solution.py:365
  5.3 5.2 %collective-permute-start = (bf16[144,128]{1,0:T(8,128)(2,1)S(1)}, bf16[144,128]{1,0:T(8,128)(2,1)S(1)}, u32[]{:S(2)}, u32[]{:S(2)}) collective-permute-start(bf16[144,128]{1,0:T(8,128)(2,1)S(1)} %get-tuple-element.17), channel_id=1, source_target_pairs={{0,29},{1,28},{2,31},{3,30},{4,9},{5,8},{6,11},{7,10},{8,5},{9,4},... | collective-permute-start | bytes 110600 | tf_op jit(solution)/shard_map/ppermute | solution.py:365
  6.9 5.2 %collective-permute-start.1 = (bf16[144,128]{1,0:T(8,128)(2,1)S(1)}, bf16[144,128]{1,0:T(8,128)(2,1)S(1)}, u32[]{:S(2)}, u32[]{:S(2)}) collective-permute-start(bf16[144,128]{1,0:T(8,128)(2,1)S(1)} %get-tuple-element.18), channel_id=1, source_target_pairs={{0,7},{1,6},{2,5},{3,4},{4,3},{5,2},{6,1},{7,0},{8,15},{9,14},{10,... | collective-permute-start | bytes 110600 | tf_op jit(solution)/shard_map/ppermute | solution.py:365
  7.8 4.3 %copy-start.2 = (s32[1,2]{1,0:T(1,128)S(1)}, s32[1,2]{1,0:T(1,128)}, u32[]{:S(2)}) copy-start(s32[1,2]{1,0:T(1,128)} %refs_0_.1) | copy-start | bytes 28
  7.8 4.3 %copy-start.3 = (s32[288,1152]{1,0:T(8,128)S(1)}, s32[288,1152]{1,0:T(8,128)}, u32[]{:S(2)}) copy-start(s32[288,1152]{1,0:T(8,128)} %refs_2_.1) | copy-start | bytes 3981316
  7.8 4.3 %copy-start.4 = (bf16[9,256,128]{2,1,0:T(8,128)(2,1)S(1)}, bf16[9,256,128]{2,1,0:T(8,128)(2,1)}, u32[]{:S(2)}) copy-start(bf16[9,256,128]{2,1,0:T(8,128)(2,1)} %constant.17.clone.refs_5_) | copy-start | bytes 1769476
  7.8 4.3 %copy-start.5 = (bf16[9,128,256]{2,1,0:T(8,128)(2,1)S(1)}, bf16[9,128,256]{2,1,0:T(8,128)(2,1)}, u32[]{:S(2)}) copy-start(bf16[9,128,256]{2,1,0:T(8,128)(2,1)} %constant.16.clone.refs_4_) | copy-start | bytes 1769476
  7.8 4.4 %copy-start.6 = (bf16[4,128,128]{2,1,0:T(8,128)(2,1)S(1)}, bf16[4,128,128]{2,1,0:T(8,128)(2,1)}, u32[]{:S(2)}) copy-start(bf16[4,128,128]{2,1,0:T(8,128)(2,1)} %constant.18.clone.refs_6_) | copy-start | bytes 393220
  8.9 19.7 %copy-start = (bf16[128,1152]{1,0:T(8,128)(2,1)S(1)}, bf16[128,1152]{1,0:T(8,128)(2,1)}, u32[]{:S(2)}) copy-start(bf16[128,1152]{1,0:T(8,128)(2,1)} %constant.19.clone.back) | copy-start | bytes 884740
  8.9 23.0 %copy-start.1 = (bf16[4,128,128]{2,1,0:T(8,128)(2,1)S(1)}, bf16[4,128,128]{2,1,0:T(8,128)(2,1)}, u32[]{:S(2)}) copy-start(bf16[4,128,128]{2,1,0:T(8,128)(2,1)} %constant.20.clone.margins) | copy-start | bytes 393220
  17.3 3.9 %collective-permute-start.3 = (bf16[64,128]{1,0:T(8,128)(2,1)S(1)}, bf16[64,128]{1,0:T(8,128)(2,1)S(1)}, u32[]{:S(2)}, u32[]{:S(2)}) collective-permute-start(bf16[64,128]{1,0:T(8,128)(2,1)S(1)} %fields.1.refs_0_), channel_id=1, source_target_pairs={{0,1},{1,0},{2,3},{3,2},{4,5},{5,4},{6,7},{7,6},{8,9},{9,8},{10,11... | collective-permute-start | bytes 49160 | tf_op jit(solution)/shard_map/ppermute | solution.py:400
  21.3 4.6 %collective-permute-start.4 = (bf16[64,128]{1,0:T(8,128)(2,1)S(1)}, bf16[64,128]{1,0:T(8,128)(2,1)S(1)}, u32[]{:S(2)}, u32[]{:S(2)}) collective-permute-start(bf16[64,128]{1,0:T(8,128)(2,1)S(1)} %total.2.refs_0_), channel_id=1, source_target_pairs={{0,2},{1,3},{2,0},{3,1},{4,6},{5,7},{6,4},{7,5},{8,10},{9,11},{10,... | collective-permute-start | bytes 49160 | tf_op jit(solution)/shard_map/ppermute | solution.py:400
  25.9 5.9 %collective-permute-start.6 = (bf16[64,128]{1,0:T(8,128)(2,1)S(1)}, bf16[64,128]{1,0:T(8,128)(2,1)S(1)}, u32[]{:S(2)}, u32[]{:S(2)}) collective-permute-start(bf16[64,128]{1,0:T(8,128)(2,1)S(1)} %total.3.own), channel_id=1, source_target_pairs={{4,8},{8,4},{12,16},{16,12},{20,24},{24,20},{5,9},{9,5},{13,17},{1... | collective-permute-start | bytes 49160 | tf_op jit(solution)/shard_map/ppermute | solution.py:409
  27.9 4.0 %collective-permute-start.5 = (bf16[64,128]{1,0:T(8,128)(2,1)S(1)}, bf16[64,128]{1,0:T(8,128)(2,1)S(1)}, u32[]{:S(2)}, u32[]{:S(2)}) collective-permute-start(bf16[64,128]{1,0:T(8,128)(2,1)S(1)} %total.3.own), channel_id=1, source_target_pairs={{0,4},{4,0},{8,12},{12,8},{16,20},{20,16},{24,28},{28,24},{1,5},{5... | collective-permute-start | bytes 49160 | tf_op jit(solution)/shard_map/ppermute | solution.py:407
